TPU v7x, 128 devices: a whole 4x4x4 slice. The times are simulated.
128 devices in a mesh: dp: 4 (over y), seq: 32 (over x, z, core).
Axes of the slice: x: 4, y: 4, z: 4, core: 2. Of those that a mesh axis runs over, the one named last changes fastest.
Arguments:
- tokens: bfloat16 [4, 16384, 1024], P('dp', 'seq'), may hold values from -18 to 18
- lengths: int32 [4, 128], P('dp'), may hold values from 1 to 128
- w_query: bfloat16 [1024, 512], replicated, may hold values from -0.1875 to 0.1875
- w_key: bfloat16 [1024, 512], replicated, may hold values from -0.1875 to 0.1875
- w_value: bfloat16 [1024, 512], replicated, may hold values from -0.1875 to 0.1875
- w_out: bfloat16 [512, 1024], replicated, may hold values from -2 to 2
- cotangent: bfloat16 [4, 16384, 1024], P('dp', 'seq'), may hold values from -6 to 6
Outputs:
- mixed: bfloat16 [4, 16384, 1024], P('dp', 'seq')
- grad_tokens: bfloat16 [4, 16384, 1024], P('dp', 'seq')
- grad_query: float32 [1024, 512], replicated
- grad_key: float32 [1024, 512], replicated
- grad_value: float32 [1024, 512], replicated
- grad_output: float32 [512, 1024], replicated
All inputs are finite; a program needn't handle non-finite values.
Results may differ from a plain program's by a relative error of at most 0.014.
The roundings to bfloat16 on the way count: a program that leaves them out, or rounds other values in their place, can miss the bound.
Values may be sent and summed in bfloat16 or wider, within the bound.
A program may use at most 192 MiB of HBM per device.

v0:
```python
import math

import jax
import jax.numpy as jnp
from jax import lax
from jax.sharding import PartitionSpec as P

HEADS = 4
TILE = 128


bar_offsets = (0, 1, 2, 4, 8, 12, 16, 24, 32)
group_bars = 4
far_score = -1e30


def sent_to_all(shard, axis):
    count = lax.axis_size(axis)
    return lax.all_to_all(
        jnp.broadcast_to(shard[None], (count, *shard.shape)), axis, 0, 0, tiled=True
    )


def joined_along(parts, dim):
    parts = jnp.moveaxis(parts, 0, dim)
    shape = parts.shape
    return parts.reshape(*shape[:dim], shape[dim] * shape[dim + 1], *shape[dim + 2 :])


def collect(shard, axis, dim):
    parts = sent_to_all(shard, axis)
    return joined_along(parts, dim)


def side_by_side(arrays, axis, dim, along):
    both = jnp.concatenate(arrays, axis=along)
    whole, at, gathered = (collect(both, axis, dim), 0, [])
    for a in arrays:
        gathered.append(lax.slice_in_dim(whole, at, at + a.shape[along], axis=along))
        at += a.shape[along]
    return tuple(gathered)


def shifted(block, axis, distance):
    devices = range(lax.axis_size(axis))
    route = [(i - distance, i) for i in devices if i - distance in devices]
    return lax.ppermute(block, axis, route)


def split_up(shard, dim, count):
    shape = shard.shape
    parts = shard.reshape(*shape[:dim], count, shape[dim] // count, *shape[dim + 1 :])
    return jnp.moveaxis(parts, dim, 0)


def sent_and_summed(shard, axis, dim):
    parts = split_up(shard, dim, lax.axis_size(axis))
    arrived = lax.all_to_all(parts, axis, split_axis=0, concat_axis=0, tiled=True)
    return arrived.astype(jnp.float32).sum(axis=0)


def in_one_piece(arrays, axis, dim, along):
    ends, at = ([], 0)
    for a in arrays[:-1]:
        at += a.shape[along]
        ends.append(at)
    both = jnp.concatenate(arrays, axis=along)
    return tuple(jnp.split(sent_and_summed(both, axis, dim), ends, axis=along))


def product(form, left, right):
    return jnp.einsum(form, left, right, preferred_element_type=jnp.float32)


def summarize(bar_rows, length):
    slot_ids = jnp.arange(bar_rows.shape[1], dtype=jnp.int32)
    live_slots = slot_ids[None, :] < length[:, None]
    running = jnp.sum(jnp.where(live_slots[:, :, None], bar_rows.astype(jnp.float32), 0.0), axis=1)
    return (running / length[:, None].astype(jnp.float32)).astype(jnp.bfloat16)


def bar_block(
    queries,
    ext_key,
    ext_value,
    ext_length,
    base_bar,
    bar_ids,
    query_length,
    summary_key,
    summary_value,
    grad_context,
):
    group_count, tile_len, head_count, head_dim = queries.shape
    sources = len(bar_offsets)
    key_parts = []
    value_parts = []
    length_parts = []
    for offset in bar_offsets:
        first_bar = base_bar - offset
        key_parts.append(lax.dynamic_slice_in_dim(ext_key, first_bar, group_count, 0))
        value_parts.append(lax.dynamic_slice_in_dim(ext_value, first_bar, group_count, 0))
        length_parts.append(lax.dynamic_slice_in_dim(ext_length, first_bar, group_count, 0))
    fine_key = jnp.stack(key_parts, 1).reshape(
        group_count, sources * tile_len, head_count, head_dim
    )
    fine_value = jnp.stack(value_parts, 1).reshape(
        group_count, sources * tile_len, head_count, head_dim
    )
    fine_length = jnp.stack(length_parts, 1)
    slot_ids = jnp.arange(tile_len, dtype=jnp.int32)
    key_live = slot_ids[None, None, :] < fine_length[:, :, None]
    causal = slot_ids[None, :] <= slot_ids[:, None]
    other_bar = jnp.arange(sources, dtype=jnp.int32) != 0
    fine_live = key_live[:, None, :, :] & (
        causal[None, :, None, :] | other_bar[None, None, :, None]
    )
    fine_live = fine_live.reshape(group_count, 1, tile_len, sources * tile_len)
    distance = bar_ids[:, None] - jnp.arange(summary_key.shape[0], dtype=jnp.int32)[None, :]
    coarse_live = distance >= 1
    for offset in bar_offsets[1:]:
        coarse_live = coarse_live & (distance != offset)
    coarse_live = coarse_live[:, None, None, :]
    score_scale = 1.0 / math.sqrt(head_dim)
    fine_score = product("gqhe,gkhe->ghqk", queries, fine_key) * score_scale
    coarse_score = product("gqhe,nhe->ghqn", queries, summary_key) * score_scale
    fine_score = jnp.where(fine_live, fine_score, far_score)
    coarse_score = jnp.where(coarse_live, coarse_score, far_score)
    top_score = jnp.maximum(jnp.max(fine_score, axis=-1), jnp.max(coarse_score, axis=-1))[..., None]
    fine_exp = jnp.where(fine_live, jnp.exp(fine_score - top_score), 0.0)
    coarse_exp = jnp.where(coarse_live, jnp.exp(coarse_score - top_score), 0.0)
    denominator = (jnp.sum(fine_exp, axis=-1) + jnp.sum(coarse_exp, axis=-1))[..., None]
    fine_prob = fine_exp / denominator
    coarse_prob = coarse_exp / denominator
    fine_round = fine_prob.astype(jnp.bfloat16)
    coarse_round = coarse_prob.astype(jnp.bfloat16)
    attended_context = product("ghqk,gkhe->gqhe", fine_round, fine_value) + product(
        "ghqn,nhe->gqhe", coarse_round, summary_value
    )
    query_live = slot_ids[None, :] < query_length[:, None]
    attended_context = jnp.where(query_live[:, :, None, None], attended_context, 0.0)
    fine_dp = product("gqhe,gkhe->ghqk", grad_context, fine_value)
    coarse_dp = product("gqhe,nhe->ghqn", grad_context, summary_value)
    delta = (jnp.sum(fine_prob * fine_dp, axis=-1) + jnp.sum(coarse_prob * coarse_dp, axis=-1))[
        ..., None
    ]
    fine_ds = (fine_prob * (fine_dp - delta) * score_scale).astype(jnp.bfloat16)
    coarse_ds = (coarse_prob * (coarse_dp - delta) * score_scale).astype(jnp.bfloat16)
    query_gradient_rows = product("ghqk,gkhe->gqhe", fine_ds, fine_key) + product(
        "ghqn,nhe->gqhe", coarse_ds, summary_key
    )
    fine_gk = product("ghqk,gqhe->gkhe", fine_ds, queries).reshape(
        group_count, sources, tile_len, head_count, head_dim
    )
    fine_gv = product("ghqk,gqhe->gkhe", fine_round, grad_context).reshape(
        group_count, sources, tile_len, head_count, head_dim
    )
    coarse_key_gradient = product("ghqn,gqhe->nhe", coarse_ds, queries)
    coarse_value_gradient = product("ghqn,gqhe->nhe", coarse_round, grad_context)
    return (
        attended_context,
        query_gradient_rows,
        fine_gk,
        fine_gv,
        coarse_key_gradient,
        coarse_value_gradient,
    )


def spread(running, grads, base_bar):
    group_count = grads.shape[0]
    for position, offset in enumerate(bar_offsets):
        first_bar = base_bar - offset
        current = lax.dynamic_slice_in_dim(running, first_bar, group_count, 0)
        running = lax.dynamic_update_slice_in_dim(
            running, current + grads[:, position], first_bar, 0
        )
    return running


def local(tokens, lengths, w_query, w_key, w_value, w_out, cotangent):
    inputs = tokens[0]
    grad_out = cotangent[0]
    token_count = inputs.shape[0]
    inner_width = w_query.shape[1]
    head_dim = inner_width // HEADS
    bar_count = token_count // TILE
    reach_dev = max(bar_offsets[-1] // bar_count, 1)
    queries = jnp.dot(inputs, w_query, preferred_element_type=jnp.float32).astype(jnp.bfloat16)
    keys_own = jnp.dot(inputs, w_key, preferred_element_type=jnp.float32).astype(jnp.bfloat16)
    values_own = jnp.dot(inputs, w_value, preferred_element_type=jnp.float32).astype(jnp.bfloat16)
    all_length = lengths[0]
    first_own = lax.axis_index("seq") * bar_count
    local_length = lax.dynamic_slice_in_dim(all_length, first_own, bar_count, 0)
    slot_ids = jnp.arange(TILE, dtype=jnp.int32)
    live_slots = slot_ids[None, :] < local_length[:, None]
    token_live = live_slots.reshape(-1)
    own_summary = (
        summarize(keys_own.reshape(bar_count, TILE, inner_width), local_length),
        summarize(values_own.reshape(bar_count, TILE, inner_width), local_length),
    )
    summary_key, summary_value = side_by_side((own_summary[0], own_summary[1]), "seq", 0, 1)
    summary_key = summary_key.reshape(-1, HEADS, head_dim)
    summary_value = summary_value.reshape(-1, HEADS, head_dim)
    grad_context = jnp.dot(grad_out, w_out.T, preferred_element_type=jnp.float32)
    grad_context = jnp.where(token_live[:, None], grad_context, 0.0).astype(jnp.bfloat16)
    key_list = [keys_own]
    value_list = [values_own]
    for distance in range(1, reach_dev + 1):
        arrived = shifted((keys_own, values_own), "seq", distance)
        key_list.append(arrived[0])
        value_list.append(arrived[1])
    key_stack = jnp.stack(key_list, 0)
    value_stack = jnp.stack(value_list, 0)
    ext_bars = (reach_dev + 1) * bar_count
    ext_key = key_stack[::-1].reshape(ext_bars, TILE, HEADS, head_dim)
    ext_value = value_stack[::-1].reshape(ext_bars, TILE, HEADS, head_dim)
    padded_length = jnp.concatenate([jnp.zeros((reach_dev * bar_count,), jnp.int32), all_length], 0)
    ext_length = lax.dynamic_slice_in_dim(padded_length, first_own, ext_bars, 0)
    query_bars = queries.reshape(bar_count, TILE, HEADS, head_dim)
    grad_bars = grad_context.reshape(bar_count, TILE, HEADS, head_dim)

    def step(carried_state, block_index):
        accumulated_key, accumulated_value, accumulated_summary_key, accumulated_summary_value = (
            carried_state
        )
        begin_bar = block_index * group_bars
        base_bar = reach_dev * bar_count + begin_bar
        bar_ids = first_own + begin_bar + jnp.arange(group_bars, dtype=jnp.int32)
        result = bar_block(
            query_bars,
            ext_key,
            ext_value,
            ext_length,
            base_bar,
            bar_ids,
            local_length,
            summary_key,
            summary_value,
            grad_bars,
        )
        (
            attended_context,
            query_gradient_rows,
            fine_gk,
            fine_gv,
            coarse_key_gradient,
            coarse_value_gradient,
        ) = result
        accumulated_key = spread(accumulated_key, fine_gk, base_bar)
        accumulated_value = spread(accumulated_value, fine_gv, base_bar)
        return (
            (
                accumulated_key,
                accumulated_value,
                accumulated_summary_key + coarse_key_gradient,
                accumulated_summary_value + coarse_value_gradient,
            ),
            (attended_context.astype(jnp.bfloat16), query_gradient_rows.astype(jnp.bfloat16)),
        )

    ext_zero = jnp.zeros((ext_bars, TILE, HEADS, head_dim), jnp.float32)
    sum_zero = jnp.zeros(summary_key.shape, jnp.float32)
    carried_state, stacked = lax.scan(
        step,
        (ext_zero, ext_zero, sum_zero, sum_zero),
        jnp.arange(bar_count // group_bars, dtype=jnp.int32),
    )
    accumulated_key, accumulated_value, accumulated_summary_key, accumulated_summary_value = (
        carried_state
    )
    attended_context = stacked[0].reshape(token_count, inner_width)
    query_gradient_rows = stacked[1].reshape(token_count, inner_width)
    grad_key_stack = accumulated_key.reshape(reach_dev + 1, token_count, inner_width)[::-1]
    grad_value_stack = accumulated_value.reshape(reach_dev + 1, token_count, inner_width)[::-1]
    own_key = grad_key_stack[0]
    own_value = grad_value_stack[0]
    for distance in range(1, reach_dev + 1):
        returned = (
            shifted(grad_key_stack[distance].astype(jnp.bfloat16), "seq", -distance).astype(
                jnp.float32
            ),
            shifted(grad_value_stack[distance].astype(jnp.bfloat16), "seq", -distance).astype(
                jnp.float32
            ),
        )
        own_key = own_key + returned[0]
        own_value = own_value + returned[1]
    summary_back = in_one_piece(
        (
            accumulated_summary_key.astype(jnp.bfloat16),
            accumulated_summary_value.astype(jnp.bfloat16),
        ),
        "seq",
        0,
        1,
    )
    inverse_denominator = 1.0 / local_length.astype(jnp.float32)
    shared_key_rows = summary_back[0].reshape(bar_count, inner_width) * inverse_denominator[:, None]
    share_value = summary_back[1].reshape(bar_count, inner_width) * inverse_denominator[:, None]
    own_key = own_key.reshape(bar_count, TILE, inner_width) + jnp.where(
        live_slots[:, :, None], shared_key_rows[:, None, :], 0.0
    )
    own_value = own_value.reshape(bar_count, TILE, inner_width) + jnp.where(
        live_slots[:, :, None], share_value[:, None, :], 0.0
    )
    grad_keys = own_key.reshape(token_count, inner_width).astype(jnp.bfloat16)
    grad_values = own_value.reshape(token_count, inner_width).astype(jnp.bfloat16)
    mixed = jnp.dot(attended_context, w_out, preferred_element_type=jnp.float32).astype(
        jnp.bfloat16
    )
    grad_in = (
        product("te,de->td", query_gradient_rows, w_query)
        + product("te,de->td", grad_keys, w_key)
        + product("te,de->td", grad_values, w_value)
    )
    weight_terms = (
        product("td,te->de", inputs, query_gradient_rows),
        product("td,te->de", inputs, grad_keys),
        product("td,te->de", inputs, grad_values),
        product("te,td->ed", attended_context, grad_out),
    )
    summed = (
        lax.psum(weight_terms[0].astype(jnp.bfloat16), ("dp", "seq")).astype(jnp.float32),
        lax.psum(weight_terms[1].astype(jnp.bfloat16), ("dp", "seq")).astype(jnp.float32),
        lax.psum(weight_terms[2].astype(jnp.bfloat16), ("dp", "seq")).astype(jnp.float32),
        lax.psum(weight_terms[3].astype(jnp.bfloat16), ("dp", "seq")).astype(jnp.float32),
    )
    return (
        mixed[None],
        grad_in.astype(jnp.bfloat16)[None],
        summed[0],
        summed[1],
        summed[2],
        summed[3],
    )


def solution(mesh):
    placed = (P("dp", "seq", None), P("dp", None), P(), P(), P(), P(), P("dp", "seq", None))
    return jax.shard_map(
        local,
        mesh=mesh,
        in_specs=placed,
        out_specs=(P("dp", "seq", None), P("dp", "seq", None), P(), P(), P(), P()),
        check_vma=False,
    )
```

profile of v0, /device:TPU:1, one launch (start us, length us, event | category | flops | bytes accessed | tf_op | source)
XLA Modules:
  0.0 742.3 jit_solution(1753987246523534247)
XLA Ops:
  11.3 4.9 collective-permute-start.15
  20.2 5.3 collective-permute-start.10
  37.1 4.8 all-to-all-start
  56.2 21.3 %all-to-all-done = bf16[32,4,1024]{2,1,0:T(4,128)(2,1)S(1)} async-done(((bf16[32,4,1024]{2,1,0:T(4,128)(2,1)}), bf16[32,4,1024]{2,1,0:T(4,128)(2,1)S(1)}, u32[]{:S(2)}, u32[]{:S(2)}) %all-to-all-start) | async-done | bytes 262176 | tf_op jit(solution)/shard_map/all_to_all | solution.py:19
  95.5 4.8 collective-permute-start.7
  101.1 11.5 %collective-permute-done.12 = bf16[512,512]{1,0:T(8,128)(2,1)S(1)} collective-permute-done((bf16[512,512]{1,0:T(8,128)(2,1)}, bf16[512,512]{1,0:T(8,128)(2,1)S(1)}, u32[]{:S(2)}, u32[]{:S(2)}) %collective-permute-start.12) | collective-permute-done | bytes 524320 | tf_op jit(solution)/shard_map/ppermute | solution.py:47
  118.3 6.4 collective-permute-start.4
  125.5 5.2 collective-permute-start.1
  141.1 7.7 %reshape.379 = bf16[36,128,4,128]{3,2,1,0:T(4,128)(2,1)} reshape(bf16[9,512,512]{2,1,0:T(8,128)(2,1)} %rev.9) | data formatting | bytes 9437184 | tf_op jit(solution)/shard_map/reshape | solution.py:216
  159.1 25.7 %collective-permute-start.3 = (bf16[512,512]{1,0:T(8,128)(2,1)}, bf16[512,512]{1,0:T(8,128)(2,1)}, u32[]{:S(2)}, u32[]{:S(2)}) collective-permute-start(bf16[512,512]{1,0:T(8,128)(2,1)} %get-tuple-element.136), channel_id=1, source_target_pairs={{0,4},{1,5},{2,6},{3,7},{4,8},{5,9},{6,10},{7,11},{8,12},{9,13},{1... | collective-permute-start | bytes 1572872 | tf_op jit(solution)/shard_map/ppermute | solution.py:47
  216.6 5.7 copy.316
  227.9 4.9 rev.8
  232.7 7.7 %reshape.376 = bf16[36,128,4,128]{3,2,1,0:T(4,128)(2,1)} reshape(bf16[9,512,512]{2,1,0:T(8,128)(2,1)} %rev.8) | data formatting | bytes 9437184 | tf_op jit(solution)/shard_map/reshape | solution.py:217
  276.0 10.1 %fusion.16 = f32[4,128,4,128]{1,3,2,0:T(8,128)} fusion(bf16[4,1152,4,128]{3,1,2,0:T(8,128)(2,1)} %bitcast.13, f32[4,4,128,1152]{3,2,1,0:T(8,128)} %copy-done.1, f32[4,4,128]{2,1,0:T(4,128)S(1)} %copy_add_fusion.1, f32[4,4,128]{2,1,0:T(4,128)S(1)} %copy_maximum_fusion, pred[4,128,1152]{2,1,0:T(8,128)(4,1)S(1)} %broadcast_and_fusion), kind=kOutput, calls=%fused_computation.36 | convolution fusion | flops 618135552 | bytes 15810560 | tf_op jit(solution)/shard_map/while/body/eval_jaxpr/ghqk,gkhe->gqhe/dot_general | solution.py:72
  286.1 6.9 multiply_reduce_fusion
  293.1 5.9 convolution_bitcast_fusion
  306.5 4.9 convolution_bitcast_fusion.1
  311.4 9.6 %copy.338 = f32[4,1152,4,128]{3,1,2,0:T(8,128)} copy(f32[4,1152,4,128]{1,3,2,0:T(8,128)} %convolution_bitcast_fusion.1) | data formatting | bytes 18874368 | tf_op jit(solution)/shard_map/while/body/eval_jaxpr/ghqk,gqhe->gkhe/transpose | solution.py:72
  338.4 10.1 %copy.362 = f32[4,1152,4,128]{3,1,2,0:T(8,128)} copy(f32[4,1152,4,128]{1,3,2,0:T(8,128)} %convolution_bitcast_fusion) | data formatting | bytes 18874368 | tf_op jit(solution)/shard_map/while/body/eval_jaxpr/ghqk,gqhe->gkhe/transpose | solution.py:72
  354.4 14.8 %all-to-all-start.1 = ((bf16[32,4,8,128]{3,1,2,0:T(4,128)(2,1)}), bf16[32,4,8,128]{3,1,2,0:T(4,128)(2,1)S(1)}, u32[]{:S(2)}, u32[]{:S(2)}) async-start(bf16[32,4,8,128]{3,1,2,0:T(4,128)(2,1)} %copy.358), calls=%async_computation.1 | async-start | bytes 524288 | tf_op jit(solution)/shard_map/all_to_all | solution.py:58
  416.7 11.3 %collective-permute-done.22 = bf16[512,512]{1,0:T(8,128)(2,1)} collective-permute-done((bf16[512,512]{1,0:T(8,128)(2,1)}, bf16[512,512]{1,0:T(8,128)(2,1)}, u32[]{:S(2)}, u32[]{:S(2)}) %collective-permute-start.22) | collective-permute-done | bytes 524320 | tf_op jit(solution)/shard_map/ppermute | solution.py:47
  431.3 18.0 %collective-permute-done.23 = bf16[512,512]{1,0:T(8,128)(2,1)} collective-permute-done((bf16[512,512]{1,0:T(8,128)(2,1)}, bf16[512,512]{1,0:T(8,128)(2,1)}, u32[]{:S(2)}, u32[]{:S(2)}) %collective-permute-start.23) | collective-permute-done | bytes 524320 | tf_op jit(solution)/shard_map/ppermute | solution.py:47
  474.5 48.7 %collective-permute-done.30 = bf16[512,512]{1,0:T(8,128)(2,1)} collective-permute-done((bf16[512,512]{1,0:T(8,128)(2,1)}, bf16[512,512]{1,0:T(8,128)(2,1)}, u32[]{:S(2)}, u32[]{:S(2)}) %collective-permute-start.30) | collective-permute-done | bytes 524320 | tf_op jit(solution)/shard_map/ppermute | solution.py:47
  548.1 178.6 %all-reduce.6.cloned.1.call-done = (bf16[1024,512]{0,1:T(8,128)(2,1)}, bf16[1024,512]{0,1:T(8,128)(2,1)}, bf16[1024,512]{0,1:T(8,128)(2,1)}, bf16[512,1024]{1,0:T(8,128)(2,1)}) async-done(((bf16[1024,512]{0,1:T(8,128)(2,1)}, bf16[1024,512]{0,1:T(8,128)(2,1)}, bf16[1024,512]{0,1:T(8,128)(2,1)}, bf16[512,1024]{1,0:T(8,128)(2,1)}), (bf16[1024,512]{0,1:T(8,128)(2,1)}, bf16[1024,512]{0,1:T(8,128)(2,1)}, ...) | async-done | bytes 4194320 | tf_op jit(solution)/shard_map/psum | solution.py:324
  (338 shorter events, 292.2 us)
Async XLA Ops:
  11.3 121.3 %collective-permute-start.15 = (bf16[512,512]{1,0:T(8,128)(2,1)}, bf16[512,512]{1,0:T(8,128)(2,1)}, u32[]{:S(2)}, u32[]{:S(2)}) collective-permute-start(bf16[512,512]{1,0:T(8,128)(2,1)} %get-tuple-element.138), channel_id=1, source_target_pairs={{0,8},{1,9},{2,10},{3,11},{4,12},{5,13},{6,14},{7,15},{8,16},{9,17... | collective-permute-start | bytes 1572872 | tf_op jit(solution)/shard_map/ppermute | solution.py:47
  16.2 109.3 %collective-permute-start.14 = (bf16[512,512]{1,0:T(8,128)(2,1)}, bf16[512,512]{1,0:T(8,128)(2,1)}, u32[]{:S(2)}, u32[]{:S(2)}) collective-permute-start(bf16[512,512]{1,0:T(8,128)(2,1)} %get-tuple-element.138), channel_id=1, source_target_pairs={{0,7},{1,8},{2,9},{3,10},{4,11},{5,12},{6,13},{7,14},{8,15},{9,16}... | collective-permute-start | bytes 1572872 | tf_op jit(solution)/shard_map/ppermute | solution.py:47
  20.2 71.2 %collective-permute-start.10 = (bf16[512,512]{1,0:T(8,128)(2,1)}, bf16[512,512]{1,0:T(8,128)(2,1)}, u32[]{:S(2)}, u32[]{:S(2)}) collective-permute-start(bf16[512,512]{1,0:T(8,128)(2,1)} %get-tuple-element.138), channel_id=1, source_target_pairs={{0,3},{1,4},{2,5},{3,6},{4,7},{5,8},{6,9},{7,10},{8,11},{9,12},{10... | collective-permute-start | bytes 1572872 | tf_op jit(solution)/shard_map/ppermute | solution.py:47
  25.5 59.8 %collective-permute-start.9 = (bf16[512,512]{1,0:T(8,128)(2,1)}, bf16[512,512]{1,0:T(8,128)(2,1)}, u32[]{:S(2)}, u32[]{:S(2)}) collective-permute-start(bf16[512,512]{1,0:T(8,128)(2,1)} %get-tuple-element.138), channel_id=1, source_target_pairs={{0,2},{1,3},{2,4},{3,5},{4,6},{5,7},{6,8},{7,9},{8,10},{9,11},{10,... | collective-permute-start | bytes 1572872 | tf_op jit(solution)/shard_map/ppermute | solution.py:47
  28.4 52.4 %collective-permute-start.8 = (bf16[512,512]{1,0:T(8,128)(2,1)}, bf16[512,512]{1,0:T(8,128)(2,1)}, u32[]{:S(2)}, u32[]{:S(2)}) collective-permute-start(bf16[512,512]{1,0:T(8,128)(2,1)} %get-tuple-element.138), channel_id=1, source_target_pairs={{0,1},{1,2},{2,3},{3,4},{4,5},{5,6},{6,7},{7,8},{8,9},{9,10},{10,1... | collective-permute-start | bytes 1572872 | tf_op jit(solution)/shard_map/ppermute | solution.py:47
  37.1 40.4 %all-to-all-start = ((bf16[32,4,1024]{2,1,0:T(4,128)(2,1)}), bf16[32,4,1024]{2,1,0:T(4,128)(2,1)S(1)}, u32[]{:S(2)}, u32[]{:S(2)}) async-start(bf16[32,4,1024]{2,1,0:T(4,128)(2,1)} %broadcast_in_dim.191), calls=%async_computation | async-start | bytes 524288 | tf_op jit(solution)/shard_map/all_to_all | solution.py:19
  95.5 130.5 %collective-permute-start.7 = (bf16[512,512]{1,0:T(8,128)(2,1)}, bf16[512,512]{1,0:T(8,128)(2,1)}, u32[]{:S(2)}, u32[]{:S(2)}) collective-permute-start(bf16[512,512]{1,0:T(8,128)(2,1)} %get-tuple-element.136), channel_id=1, source_target_pairs={{0,8},{1,9},{2,10},{3,11},{4,12},{5,13},{6,14},{7,15},{8,16},{9,17... | collective-permute-start | bytes 1572872 | tf_op jit(solution)/shard_map/ppermute | solution.py:47
  112.6 111.5 %collective-permute-start.6 = (bf16[512,512]{1,0:T(8,128)(2,1)}, bf16[512,512]{1,0:T(8,128)(2,1)}, u32[]{:S(2)}, u32[]{:S(2)}) collective-permute-start(bf16[512,512]{1,0:T(8,128)(2,1)} %get-tuple-element.136), channel_id=1, source_target_pairs={{0,7},{1,8},{2,9},{3,10},{4,11},{5,12},{6,13},{7,14},{8,15},{9,16}... | collective-permute-start | bytes 1572872 | tf_op jit(solution)/shard_map/ppermute | solution.py:47
  118.3 78.3 %collective-permute-start.4 = (bf16[512,512]{1,0:T(8,128)(2,1)}, bf16[512,512]{1,0:T(8,128)(2,1)}, u32[]{:S(2)}, u32[]{:S(2)}) collective-permute-start(bf16[512,512]{1,0:T(8,128)(2,1)} %get-tuple-element.136), channel_id=1, source_target_pairs={{0,5},{1,6},{2,7},{3,8},{4,9},{5,10},{6,11},{7,12},{8,13},{9,14},{... | collective-permute-start | bytes 1572872 | tf_op jit(solution)/shard_map/ppermute | solution.py:47
  154.8 35.8 %collective-permute-start.2 = (bf16[512,512]{1,0:T(8,128)(2,1)}, bf16[512,512]{1,0:T(8,128)(2,1)}, u32[]{:S(2)}, u32[]{:S(2)}) collective-permute-start(bf16[512,512]{1,0:T(8,128)(2,1)} %get-tuple-element.136), channel_id=1, source_target_pairs={{0,3},{1,4},{2,5},{3,6},{4,7},{5,8},{6,9},{7,10},{8,11},{9,12},{10... | collective-permute-start | bytes 1572872 | tf_op jit(solution)/shard_map/ppermute | solution.py:47
  354.4 113.5 %all-to-all-start.1 = ((bf16[32,4,8,128]{3,1,2,0:T(4,128)(2,1)}), bf16[32,4,8,128]{3,1,2,0:T(4,128)(2,1)S(1)}, u32[]{:S(2)}, u32[]{:S(2)}) async-start(bf16[32,4,8,128]{3,1,2,0:T(4,128)(2,1)} %copy.358), calls=%async_computation.1 | async-start | bytes 524288 | tf_op jit(solution)/shard_map/all_to_all | solution.py:58
  369.2 357.5 %all-reduce.6.cloned.1.call-start = ((), (), s32[]{:S(2)}) async-start(), calls=%async_computation.2 | async-start | bytes 8388608 | tf_op jit(solution)/shard_map/psum | solution.py:324
  384.5 43.6 %collective-permute-start.22 = (bf16[512,512]{1,0:T(8,128)(2,1)}, bf16[512,512]{1,0:T(8,128)(2,1)}, u32[]{:S(2)}, u32[]{:S(2)}) collective-permute-start(bf16[512,512]{1,0:T(8,128)(2,1)} %bitcast.488), channel_id=1, source_target_pairs={{7,0},{8,1},{9,2},{10,3},{11,4},{12,5},{13,6},{14,7},{15,8},{16,9}... | collective-permute-start | bytes 1572872 | tf_op jit(solution)/shard_map/ppermute | solution.py:47
  385.8 44.2 %collective-permute-start.21 = (bf16[512,512]{1,0:T(8,128)(2,1)}, bf16[512,512]{1,0:T(8,128)(2,1)}, u32[]{:S(2)}, u32[]{:S(2)}) collective-permute-start(bf16[512,512]{1,0:T(8,128)(2,1)} %bitcast.489), channel_id=1, source_target_pairs={{6,0},{7,1},{8,2},{9,3},{10,4},{11,5},{12,6},{13,7},{14,8},{15,9},... | collective-permute-start | bytes 1572872 | tf_op jit(solution)/shard_map/ppermute | solution.py:47
  387.1 62.1 %collective-permute-start.23 = (bf16[512,512]{1,0:T(8,128)(2,1)}, bf16[512,512]{1,0:T(8,128)(2,1)}, u32[]{:S(2)}, u32[]{:S(2)}) collective-permute-start(bf16[512,512]{1,0:T(8,128)(2,1)} %bitcast.487), channel_id=1, source_target_pairs={{8,0},{9,1},{10,2},{11,3},{12,4},{13,5},{14,6},{15,7},{16,8},{17,9... | collective-permute-start | bytes 1572872 | tf_op jit(solution)/shard_map/ppermute | solution.py:47
  409.9 40.6 %collective-permute-start.18 = (bf16[512,512]{1,0:T(8,128)(2,1)S(1)}, bf16[512,512]{1,0:T(8,128)(2,1)}, u32[]{:S(2)}, u32[]{:S(2)}) collective-permute-start(bf16[512,512]{1,0:T(8,128)(2,1)S(1)} %bitcast.542), channel_id=1, source_target_pairs={{3,0},{4,1},{5,2},{6,3},{7,4},{8,5},{9,6},{10,7},{11,8},{12,9},{13... | collective-permute-start | bytes 1572872 | tf_op jit(solution)/shard_map/ppermute | solution.py:47
  415.4 52.5 %collective-permute-start.19 = (bf16[512,512]{1,0:T(8,128)(2,1)}, bf16[512,512]{1,0:T(8,128)(2,1)}, u32[]{:S(2)}, u32[]{:S(2)}) collective-permute-start(bf16[512,512]{1,0:T(8,128)(2,1)} %bitcast.491), channel_id=1, source_target_pairs={{4,0},{5,1},{6,2},{7,3},{8,4},{9,5},{10,6},{11,7},{12,8},{13,9},{1... | collective-permute-start | bytes 1572872 | tf_op jit(solution)/shard_map/ppermute | solution.py:47
  428.0 41.2 %collective-permute-start.16 = (bf16[512,512]{1,0:T(8,128)(2,1)}, bf16[512,512]{1,0:T(8,128)(2,1)}, u32[]{:S(2)}, u32[]{:S(2)}) collective-permute-start(bf16[512,512]{1,0:T(8,128)(2,1)} %bitcast.494), channel_id=1, source_target_pairs={{1,0},{2,1},{3,2},{4,3},{5,4},{6,5},{7,6},{8,7},{9,8},{10,9},{11,1... | collective-permute-start | bytes 1572872 | tf_op jit(solution)/shard_map/ppermute | solution.py:47
  430.0 42.0 %collective-permute-start.25 = (bf16[512,512]{1,0:T(8,128)(2,1)}, bf16[512,512]{1,0:T(8,128)(2,1)}, u32[]{:S(2)}, u32[]{:S(2)}) collective-permute-start(bf16[512,512]{1,0:T(8,128)(2,1)} %bitcast.485), channel_id=1, source_target_pairs={{2,0},{3,1},{4,2},{5,3},{6,4},{7,5},{8,6},{9,7},{10,8},{11,9},{12,... | collective-permute-start | bytes 1572872 | tf_op jit(solution)/shard_map/ppermute | solution.py:47
  450.5 72.7 %collective-permute-start.30 = (bf16[512,512]{1,0:T(8,128)(2,1)}, bf16[512,512]{1,0:T(8,128)(2,1)}, u32[]{:S(2)}, u32[]{:S(2)}) collective-permute-start(bf16[512,512]{1,0:T(8,128)(2,1)} %bitcast.480), channel_id=1, source_target_pairs={{7,0},{8,1},{9,2},{10,3},{11,4},{12,5},{13,6},{14,7},{15,8},{16,9}... | collective-permute-start | bytes 1572872 | tf_op jit(solution)/shard_map/ppermute | solution.py:47
  468.0 62.1 %collective-permute-start.29 = (bf16[512,512]{1,0:T(8,128)(2,1)}, bf16[512,512]{1,0:T(8,128)(2,1)S(1)}, u32[]{:S(2)}, u32[]{:S(2)}) collective-permute-start(bf16[512,512]{1,0:T(8,128)(2,1)} %bitcast.547), channel_id=1, source_target_pairs={{6,0},{7,1},{8,2},{9,3},{10,4},{11,5},{12,6},{13,7},{14,8},{15,9},... | collective-permute-start | bytes 1572872 | tf_op jit(solution)/shard_map/ppermute | solution.py:47
  469.3 63.5 %collective-permute-start.31 = (bf16[512,512]{1,0:T(8,128)(2,1)}, bf16[512,512]{1,0:T(8,128)(2,1)S(1)}, u32[]{:S(2)}, u32[]{:S(2)}) collective-permute-start(bf16[512,512]{1,0:T(8,128)(2,1)} %bitcast.546), channel_id=1, source_target_pairs={{8,0},{9,1},{10,2},{11,3},{12,4},{13,5},{14,6},{15,7},{16,8},{17,9... | collective-permute-start | bytes 1572872 | tf_op jit(solution)/shard_map/ppermute | solution.py:47
  471.9 60.8 %collective-permute-start.26 = (bf16[512,512]{1,0:T(8,128)(2,1)}, bf16[512,512]{1,0:T(8,128)(2,1)S(1)}, u32[]{:S(2)}, u32[]{:S(2)}) collective-permute-start(bf16[512,512]{1,0:T(8,128)(2,1)} %bitcast.545), channel_id=1, source_target_pairs={{3,0},{4,1},{5,2},{6,3},{7,4},{8,5},{9,6},{10,7},{11,8},{12,9},{13... | collective-permute-start | bytes 1572872 | tf_op jit(solution)/shard_map/ppermute | solution.py:47
  473.2 59.5 %collective-permute-start.27 = (bf16[512,512]{1,0:T(8,128)(2,1)}, bf16[512,512]{1,0:T(8,128)(2,1)S(1)}, u32[]{:S(2)}, u32[]{:S(2)}) collective-permute-start(bf16[512,512]{1,0:T(8,128)(2,1)} %bitcast.544), channel_id=1, source_target_pairs={{4,0},{5,1},{6,2},{7,3},{8,4},{9,5},{10,6},{11,7},{12,8},{13,9},{1... | collective-permute-start | bytes 1572872 | tf_op jit(solution)/shard_map/ppermute | solution.py:47
  (57 other events, 927.2 us)
Sparse Core Ops, SparseCore 0:
  540.7 185.9 all-reduce.5
where the time goes:
time: 754 us; the launch traced here: 742 us
  waiting for transfers between devices  300 us (40%)
  local copies, waits for them, and re-layouts  193 us (26%)
  starting transfers between devices  121 us (16%)
  matrix products  65 us (9%)
  other arithmetic  48.3 us (6%)
  between operations  15.3 us (2%)
    psum x1, waiting for transfers between devices, local(): lax.psum(weight_terms[0].astype(jnp.bfloat16), ('dp', 'seq'))  179 us
    ppermute x32, starting transfers between devices, shifted(): return lax.ppermute(block, axis, route)  101 us
    ppermute x32, waiting for transfers between devices, shifted(): return lax.ppermute(block, axis, route)  100 us
    unnamed x142, local copies, waits for them, and re-layouts  76.9 us
    dot_general x19, matrix products, product(): return jnp.einsum(form, left, right, preferred_element_type=jnp.float32)  53.9 us
    all_to_all x1, waiting for transfers between devices, sent_to_all(): lax.all_to_all(jnp.broadcast_to(shard[None], (count, *shard.shape)), axis...  21.3 us
    another operation x9, local copies, waits for them, and re-layouts, bar_block(): jnp.stack(key_parts, 1)  20.7 us
    transpose x2, local copies, waits for them, and re-layouts, product(): return jnp.einsum(form, left, right, preferred_element_type=jnp.float32)  19.7 us
  transfers between devices with their start and end apart: 35, of which 10 were waited for; matrix products, arithmetic and copies ran while one was open for 22% of the time, Pallas kernels for 0%

commit v1 on v0

v1 whole, which is shorter than its diff:
```python
import functools
import math

import jax
import jax.numpy as jnp
from jax import lax
from jax.experimental import pallas as pl
from jax.experimental.pallas import tpu as pltpu
from jax.sharding import PartitionSpec as P

MESH = pl.DeviceIdType.MESH
BF = jnp.bfloat16
F32 = jnp.float32
HEADS = 4
TILE = 128
OFFSETS = (0, 1, 2, 4, 8, 12, 16, 24, 32)
SCALE = 1.0 / math.sqrt(128.0)
LOG2E = 1.4426950408889634
NEG = -1e30
NT = (((1,), (1,)), ((), ()))
TN = (((0,), (0,)), ((), ()))
OWN = 32 * TILE
MIB = 1024 * 1024


def place():
    s = lax.axis_index("seq")
    return lax.axis_index("dp"), lax.div(s, 8), lax.rem(lax.div(s, 2), 4), lax.rem(s, 2)


def device(y, x, z, c):
    return (y, (x * 4 + z) * 2 + c)


def turn(a, d):
    return lax.rem(a + d, 4)


def remote(src, dst, send, recv, to):
    return pltpu.make_async_remote_copy(
        src_ref=src, dst_ref=dst, send_sem=send, recv_sem=recv, device_id=to, device_id_type=MESH
    )


def greet(partners):
    barrier = pltpu.get_barrier_semaphore()
    for to in partners:
        pl.semaphore_signal(barrier, inc=1, device_id=to, device_id_type=MESH)
    pl.semaphore_wait(barrier, len(partners))


def plane_partners(y, x, z, c):
    found = [device(y, x, z, 1 - c)]
    for d in (1, 2, 3):
        for core in (0, 1):
            found.append(device(y, turn(x, d), z, core))
            found.append(device(y, x, turn(z, d), core))
    return found


def rows_of(start, count):
    return pl.ds(pl.multiple_of(start, TILE), count)


def spread_kernel(
    lens, tok, cot, wq, wk, wv, wo, kv, qg, summ,
    kvs, qgs, sums, s_kv, r_kv, s_qg, r_qg, s_h, r_h, s_x, r_x, s_s, r_s,
):
    y, x, z, c = place()
    greet(plane_partners(y, x, z, c))
    other = device(y, x, z, 1 - c)
    home = lax.div(z, 2)
    slot = lax.rem(z, 2) * 2 + c
    at_home = c == home

    def project(src, w, dst, lane, mask):
        def half(i, carry):
            rows = rows_of(i * 256, 256)
            got = jnp.dot(src[rows, :], w[...], preferred_element_type=F32)
            for h in range(HEADS):
                dst[h, rows, lane : lane + TILE] = got[:, h * TILE : (h + 1) * TILE].astype(BF)
            return carry

        lax.fori_loop(0, 2, half, 0)

    def exchange(staged, landing, base, send, recv):
        spot = rows_of(base + slot * 512, 512)
        copies = []
        for d in (1, 2, 3):
            h = turn(z, d)
            copy = remote(staged.at[h], landing.at[spot], send.at[d], recv.at[slot], device(y, x, h, home))
            copy.start()
            copies.append(copy)
        near = remote(staged.at[z], landing.at[spot], send.at[0], recv.at[slot], other)

        @pl.when(at_home)
        def _():
            landing[spot, :] = staged[z]

        @pl.when(jnp.logical_not(at_home))
        def _():
            near.start()

        return copies, near

    def settle(copies, near):
        for copy in copies:
            copy.wait_send()

        @pl.when(jnp.logical_not(at_home))
        def _():
            near.wait_send()

    def arrived(staged, landing, base, send, recv, i):
        mine = jnp.logical_and(z == 2 * c + i // 2, c == i % 2)

        @pl.when(jnp.logical_not(mine))
        def _():
            remote(
                staged.at[0], landing.at[pl.ds(base + i * 512, 512)], send.at[0], recv.at[i], other
            ).wait_recv()

    project(tok, wk, kvs, 0, False)
    project(tok, wv, kvs, TILE, False)
    kv_sent = exchange(kvs, kv, OWN, s_kv, r_kv)
    project(tok, wq, qgs, 0, False)
    first_own = ((x * 4 + z) * 2 + c) * 4

    def grads(i, carry):
        rows = rows_of(i * TILE, TILE)
        got = lax.dot_general(cot[rows, :], wo[...], NT, preferred_element_type=F32)
        live = lax.broadcasted_iota(jnp.int32, (TILE, 512), 0) < lens[0, first_own + i]
        got = jnp.where(live, got, 0.0).astype(BF)
        for h in range(HEADS):
            qgs[h, rows, TILE : 2 * TILE] = got[:, h * TILE : (h + 1) * TILE]
        return carry

    lax.fori_loop(0, 4, grads, 0)
    qg_sent = exchange(qgs, qg, 0, s_qg, r_qg)

    group = 2 * x + c
    ahead = device(y, turn(x, 1), z, c)
    halos, across = [], []
    for i in range(4):
        arrived(kvs, kv, OWN, s_kv, r_kv, i)
        own = kv.at[pl.ds(OWN + i * 512, 512)]
        halo = remote(own, kv.at[pl.ds(i * 512, 512)], s_h.at[i], r_h.at[i], ahead)
        halo.start()
        halos.append(halo)
        give = remote(own, kv.at[pl.ds(2048 + i * 512, 512)], s_x.at[i], r_x.at[i], other)

        @pl.when(c == 0)
        def _():
            give.start()

    def summary(i, carry):
        rows = rows_of(OWN + i * TILE, TILE)
        length = lens[0, group * 16 + i]
        live = lax.broadcasted_iota(jnp.int32, (TILE, 256), 0) < length
        total = jnp.sum(jnp.where(live, kv[rows, :].astype(F32), 0.0), axis=0, keepdims=True)
        sums[pl.ds(i, 1), :] = total / jnp.full((1, 256), length, jnp.int32).astype(F32)
        return carry

    lax.fori_loop(0, 16, summary, 0)
    summ[group] = sums[...].astype(BF)
    sum_copies = []
    for d, cc in [(d, cc) for d in range(4) for cc in (0, 1) if (d, cc) != (0, 0)]:
        n = d * 2 + cc
        core = lax.rem(c + cc, 2)
        copy = remote(summ.at[group], summ.at[group], s_s.at[n], r_s.at[n], device(y, turn(x, d), z, core))
        copy.start()
        sum_copies.append(copy)

    for i in range(4):
        halos[i].wait_recv()
        pass_on = remote(
            kv.at[pl.ds(i * 512, 512)], kv.at[pl.ds(2048 + i * 512, 512)], s_x.at[i], r_x.at[i], other
        )

        @pl.when(c == 1)
        def _():
            pass_on.start()

        across.append(pass_on)
    for copy in across:
        copy.wait()
    for copy in halos:
        copy.wait_send()
    for i in range(4):
        arrived(qgs, qg, 0, s_qg, r_qg, i)
    for copy in sum_copies:
        copy.wait()
    settle(*kv_sent)
    settle(*qg_sent)


def attend_kernel(lens, kv, qg, summ, cg, gkv, gsum, kvt, gt, pair, sc, dsp):
    y, x, z, c = place()
    group = 2 * x + c
    pair[...] = jnp.zeros_like(pair)
    gsum[...] = jnp.zeros_like(gsum)

    def prepare(b, carry):
        rows = rows_of(b * TILE, TILE)
        kvt[:, rows] = jnp.transpose(kv[rows, :])
        gkv[rows, :] = jnp.zeros((TILE, 256), F32)
        return carry

    lax.fori_loop(0, 48, prepare, 0)
    kvt[:, 48 * TILE : 49 * TILE] = jnp.transpose(summ[...])
    key_slot = lax.broadcasted_iota(jnp.int32, (TILE, TILE), 0)
    query_slot = lax.broadcasted_iota(jnp.int32, (TILE, TILE), 1)
    count = len(OFFSETS)

    def bar(qb, carry):
        rows = rows_of(qb * TILE, TILE)
        pair[0:TILE, 0:TILE] = qg[rows, 0:TILE]
        pair[TILE:, TILE:] = qg[rows, TILE:]
        both = pair[...]
        this = 16 * group + qb
        top = None
        for j in range(count + 1):
            here = slice(j * TILE, (j + 1) * TILE)
            if j < count:
                spot = rows_of((32 + qb - OFFSETS[j]) * TILE, TILE)
                bar_id = this - OFFSETS[j]
                length = jnp.where(bar_id >= 0, lens[0, jnp.maximum(bar_id, 0)], 0)
                source = kv[spot, :]
                gt[:, here] = kvt[:, spot]
                ok = key_slot < length
                if j == 0:
                    ok = jnp.logical_and(ok, key_slot <= query_slot)
            else:
                source = summ[...]
                gt[:, here] = kvt[:, 48 * TILE : 49 * TILE]
                distance = this - key_slot
                ok = distance >= 1
                for o in OFFSETS[1:]:
                    ok = jnp.logical_and(ok, distance != o)
            got = lax.dot_general(source, both, NT, preferred_element_type=F32)
            score = jnp.where(ok, got[:, :TILE] * (SCALE * LOG2E), NEG)
            sc[here, :TILE] = score
            sc[here, TILE:] = got[:, TILE:]
            high = jnp.max(score, axis=0, keepdims=True)
            top = high if top is None else jnp.maximum(top, high)
        total = jnp.zeros((1, TILE), F32)
        weighted = jnp.zeros((1, TILE), F32)
        for j in range(count + 1):
            here = slice(j * TILE, (j + 1) * TILE)
            e = jnp.exp2(sc[here, :TILE] - top)
            sc[here, :TILE] = e
            total = total + jnp.sum(e, axis=0, keepdims=True)
            weighted = weighted + jnp.sum(e * sc[here, TILE:], axis=0, keepdims=True)
        inverse = 1.0 / total
        delta = weighted * inverse
        for j in range(count + 1):
            here = slice(j * TILE, (j + 1) * TILE)
            p = sc[here, :TILE] * inverse
            dsp[here, :TILE] = (p * (sc[here, TILE:] - delta)).astype(BF)
            dsp[here, TILE:] = p.astype(BF)
            got = jnp.dot(dsp[here, :], both, preferred_element_type=F32)
            if j < count:
                spot = rows_of((32 + qb - OFFSETS[j]) * TILE, TILE)
                gkv[spot, :] += got
            else:
                gsum[...] += got
        out = jnp.dot(gt[...], dsp[...], preferred_element_type=F32)
        cg[rows, 0:TILE] = jnp.transpose(out[:TILE, :TILE] * SCALE).astype(BF)
        context = jnp.transpose(out[TILE:, TILE:])
        cg[rows, TILE:] = jnp.where(key_slot < lens[0, this], context, 0.0).astype(BF)
        return carry

    lax.fori_loop(0, 16, bar, 0)


def back_kernel(
    lens, gkv, gsum, cg, tok, cot, wq, wk, wv, wo, mixed, gin, wg,
    sx, rx, sh, rh, gss, gsr, own, ret_kv, ret_cg, flat,
    s_kv, r_kv, s_cg, r_cg, s_h, r_h, s_x, r_x, s_s, r_s,
):
    y, x, z, c = place()
    greet(plane_partners(y, x, z, c))
    other = device(y, x, z, 1 - c)
    home = lax.div(z, 2)
    at_home = c == home
    group = 2 * x + c

    def owner(i):
        to_z = 2 * c + i // 2
        mine = jnp.logical_and(z == to_z, c == i % 2)
        return device(y, x, to_z, i % 2), mine

    def give_back(src, landing, send, recv, i):
        to, mine = owner(i)
        rows = pl.ds(i * 512, 512)

        @pl.when(mine)
        def _():
            landing[z] = src[rows, :]

        @pl.when(jnp.logical_not(mine))
        def _():
            remote(src.at[rows], landing.at[z], send.at[i], recv.at[z], to).start()

    def settle(src, landing, send, recv):
        for i in range(4):
            to, mine = owner(i)

            @pl.when(jnp.logical_not(mine))
            def _():
                remote(src.at[pl.ds(i * 512, 512)], landing.at[z], send.at[i], recv.at[z], to).wait_send()

    def returned(src, landing, send, recv):
        for h in range(HEADS):
            mine = jnp.logical_and(z == h, at_home)

            @pl.when(jnp.logical_not(mine))
            def _():
                remote(src.at[pl.ds(0, 512)], landing.at[h], send.at[0], recv.at[h], other).wait_recv()

    crossing = []
    for i in range(4):
        rows = pl.ds(i * 512, 512)
        sx[rows, :] = gkv[pl.ds(2048 + i * 512, 512), :].astype(BF)
        copy = remote(sx.at[rows], rx.at[rows], s_x.at[i], r_x.at[i], other)
        copy.start()
        crossing.append(copy)
    for i in range(4):
        give_back(cg, ret_cg, s_cg, r_cg, i)
    gss[...] = gsum[...].astype(BF).reshape(8, 16, 256)
    gsr[group] = gss[group]
    sum_copies = []
    for d, cc in [(d, cc) for d in range(4) for cc in (0, 1) if (d, cc) != (0, 0)]:
        n = d * 2 + cc
        to_x, core = turn(x, d), lax.rem(c + cc, 2)
        copy = remote(
            gss.at[to_x * 2 + core], gsr.at[group], s_s.at[n], r_s.at[n], device(y, to_x, z, core)
        )
        copy.start()
        sum_copies.append(copy)
    behind = device(y, turn(x, 3), z, c)
    halos = []
    for i in range(4):
        rows = pl.ds(i * 512, 512)
        crossing[i].wait_recv()

        @pl.when(c == 0)
        def _():
            sh[rows, :] = gkv[rows, :].astype(BF)

        @pl.when(c == 1)
        def _():
            sh[rows, :] = (gkv[rows, :] + rx[rows, :].astype(F32)).astype(BF)

        copy = remote(sh.at[rows], rh.at[rows], s_h.at[i], r_h.at[i], behind)
        copy.start()
        halos.append(copy)

    def flatten(src, lane, n):
        for h in range(HEADS):
            flat[n, :, h * TILE : (h + 1) * TILE] = src[h, :, lane : lane + TILE]

    def weight_grad(n, m):
        def part(i, carry):
            cols = rows_of(i * 256, 256)
            got = lax.dot_general(tok[:, cols], flat[n], TN, preferred_element_type=F32).astype(BF)
            wg[m, 0, cols, :] = got[:, :256]
            wg[m, 1, cols, :] = got[:, 256:]
            return carry

        lax.fori_loop(0, 4, part, 0)

    returned(cg, ret_cg, s_cg, r_cg)
    flatten(ret_cg, 0, 0)
    flatten(ret_cg, TILE, 1)

    def mix(i, carry):
        rows = rows_of(i * 256, 256)
        mixed[rows, :] = jnp.dot(flat[1, rows, :], wo[...], preferred_element_type=F32).astype(BF)
        return carry

    lax.fori_loop(0, 2, mix, 0)
    weight_grad(0, 0)

    def out_grad(i, carry):
        cols = rows_of(i * 256, 256)
        got = lax.dot_general(flat[1], cot[:, cols], TN, preferred_element_type=F32).astype(BF)
        wg[3, lax.div(i, 2), rows_of(lax.rem(i, 2) * 512, 512), :] = got
        return carry

    lax.fori_loop(0, 4, out_grad, 0)

    for copy in sum_copies:
        copy.wait()
    coarse = gsr[0].astype(F32)
    for n in range(1, 8):
        coarse = coarse + gsr[n].astype(F32)
    lane = lax.broadcasted_iota(jnp.int32, (1, 256), 1)
    factor = jnp.where(lane < TILE, SCALE, 1.0)
    for i in range(4):
        halos[i].wait_recv()
        for b in range(4 * i, 4 * i + 4):
            rows = pl.ds(b * TILE, TILE)
            length = lens[0, group * 16 + b]
            live = lax.broadcasted_iota(jnp.int32, (TILE, 256), 0) < length
            share = coarse[b : b + 1, :] * (1.0 / jnp.full((1, 256), length, jnp.int32).astype(F32))
            extra = jnp.where(c == 0, rx[rows, :].astype(F32), 0.0)
            total = gkv[pl.ds(OWN + b * TILE, TILE), :] + rh[rows, :].astype(F32) + extra
            own[rows, :] = ((total + jnp.where(live, share, 0.0)) * factor).astype(BF)
        give_back(own, ret_kv, s_kv, r_kv, i)
    returned(own, ret_kv, s_kv, r_kv)
    flatten(ret_kv, 0, 1)
    flatten(ret_kv, TILE, 2)
    weight_grad(1, 1)
    weight_grad(2, 2)

    def back(i, carry):
        rows = rows_of(i * 256, 256)
        total = lax.dot_general(flat[0, rows, :], wq[...], NT, preferred_element_type=F32)
        total = total + lax.dot_general(flat[1, rows, :], wk[...], NT, preferred_element_type=F32)
        total = total + lax.dot_general(flat[2, rows, :], wv[...], NT, preferred_element_type=F32)
        gin[rows, :] = total.astype(BF)
        return carry

    lax.fori_loop(0, 2, back, 0)
    settle(cg, ret_cg, s_cg, r_cg)
    settle(own, ret_kv, s_kv, r_kv)
    for copy in crossing + halos:
        copy.wait_send()


ORDERS = ("yxz", "xzy", "zyx", "yzx")


def reduce_kernel(wg, out, got0, w0, got1, w1, got2, w2, got3, s0, r0, s1, r1, s2, r2):
    y, x, z, c = place()
    where = {"y": y, "x": x, "z": z}

    def along(axis, d):
        at = dict(where)
        at[axis] = turn(where[axis], d)
        return device(at["y"], at["x"], at["z"], c)

    other = device(y, x, z, 1 - c)
    greet([other] + [along(axis, d) for axis in "yxz" for d in (1, 2, 3)])

    started = []
    first = []
    for m in range(4):
        copy = remote(wg.at[m, 1 - c], got0.at[m], s0.at[0, m], r0.at[0, m], other)
        copy.start()
        first.append(copy)
    sources = [None] * 4
    levels = ((w0, got1, 256), (w1, got2, 64), (w2, got3, 16))
    pending = [None] * 4

    def send_level(m, level):
        src, got, size = levels[level]
        copies = []
        axis = ORDERS[m][level]
        for d in (1, 2, 3):
            piece = pl.ds(pl.multiple_of(turn(where[axis], d) * size, 16), size)
            copy = remote(
                src.at[m, piece], got.at[m, d - 1], s1.at[level, m, d - 1], r1.at[level, m, d - 1], along(axis, d)
            )
            copy.start()
            copies.append(copy)
        return copies

    def place_rows(m, level):
        a, b, d = (where[axis] for axis in ORDERS[m])
        start = a * 256
        if level >= 1:
            start = start + b * 64
        if level >= 2:
            start = start + d * 16
        return pl.ds(pl.multiple_of(start, 16), levels[level][2])

    for m in range(4):
        first[m].wait_recv()

        def add(i, carry, m=m):
            rows = rows_of(i * 256, 256)
            w0[m, rows, :] = (wg[m, c, rows, :].astype(F32) + got0[m, rows, :].astype(F32)).astype(BF)
            return carry

        lax.fori_loop(0, 4, add, 0)
        pending[m] = send_level(m, 0)
        started += pending[m]
    for level in range(3):
        src, got, size = levels[level]
        for m in range(4):
            for copy in pending[m]:
                copy.wait_recv()
            mine = pl.ds(pl.multiple_of(where[ORDERS[m][level]] * size, 16), size)
            total = src[m, mine, :].astype(F32)
            for n in range(3):
                total = total + got[m, n].astype(F32)
            if level < 2:
                levels[level + 1][0][m] = total.astype(BF)
                pending[m] = send_level(m, level + 1)
                started += pending[m]
            else:
                out[m, c, place_rows(m, 2), :] = total.astype(BF)

    def give(m, level):
        block = out.at[m, c, place_rows(m, level)]
        copies = []
        for d in (1, 2, 3):
            copy = remote(
                block, block, s2.at[level, m, d - 1], r2.at[level, m, d - 1], along(ORDERS[m][level], d)
            )
            copy.start()
            copies.append(copy)
        return copies

    for m in range(4):
        pending[m] = give(m, 2)
        started += pending[m]
    last = []
    for level in (1, 0, None):
        for m in range(4):
            for copy in pending[m]:
                copy.wait_recv()
            if level is None:
                copy = remote(out.at[m, c], out.at[m, c], s0.at[1, m], r0.at[1, m], other)
                copy.start()
                last.append(copy)
            else:
                pending[m] = give(m, level)
                started += pending[m]
    for copy in last:
        copy.wait()
    for copy in first + started:
        copy.wait_send()


VM = pl.BlockSpec(memory_space=pltpu.VMEM)
SM = pl.BlockSpec(memory_space=pltpu.SMEM)
DMA = pltpu.SemaphoreType.DMA


def params(identity, mib):
    if identity is None:
        return pltpu.CompilerParams(vmem_limit_bytes=mib * MIB)
    return pltpu.CompilerParams(
        collective_id=identity, has_side_effects=True, vmem_limit_bytes=mib * MIB
    )


def shape(*dims, kind=BF):
    return jax.ShapeDtypeStruct(dims, kind)


def local(tokens, lengths, w_query, w_key, w_value, w_out, cotangent):
    tok, cot = tokens[0], cotangent[0]
    kv, qg, summ = pl.pallas_call(
        spread_kernel,
        out_shape=(shape(6144, 256), shape(2048, 256), shape(8, 16, 256)),
        in_specs=[SM] + [VM] * 6,
        out_specs=(VM, VM, VM),
        scratch_shapes=[
            pltpu.VMEM((4, 512, 256), BF),
            pltpu.VMEM((4, 512, 256), BF),
            pltpu.VMEM((16, 256), F32),
        ]
        + [DMA((4,))] * 8
        + [DMA((8,))] * 2,
        compiler_params=params(0, 40),
        name="spread",
    )(lengths, tok, cot, w_query, w_key, w_value, w_out)
    cg, gkv, gsum = pl.pallas_call(
        attend_kernel,
        out_shape=(shape(2048, 256), shape(6144, 256, kind=F32), shape(128, 256, kind=F32)),
        in_specs=[SM, VM, VM, VM],
        out_specs=(VM, VM, VM),
        scratch_shapes=[
            pltpu.VMEM((256, 49 * TILE), BF),
            pltpu.VMEM((256, 10 * TILE), BF),
            pltpu.VMEM((256, 256), BF),
            pltpu.VMEM((10 * TILE, 256), F32),
            pltpu.VMEM((10 * TILE, 256), BF),
        ],
        compiler_params=params(None, 40),
        name="attend",
    )(lengths, kv, qg, summ.reshape(128, 256))
    mixed, gin, wg = pl.pallas_call(
        back_kernel,
        out_shape=(shape(512, 1024), shape(512, 1024), shape(4, 2, 1024, 256)),
        in_specs=[SM] + [VM] * 9,
        out_specs=(VM, VM, VM),
        scratch_shapes=[pltpu.VMEM((2048, 256), BF)] * 4
        + [pltpu.VMEM((8, 16, 256), BF)] * 2
        + [
            pltpu.VMEM((2048, 256), BF),
            pltpu.VMEM((4, 512, 256), BF),
            pltpu.VMEM((4, 512, 256), BF),
            pltpu.VMEM((3, 512, 512), BF),
        ]
        + [DMA((4,))] * 8
        + [DMA((8,))] * 2,
        compiler_params=params(1, 48),
        name="back",
    )(lengths, gkv, gsum, cg, tok, cot, w_query, w_key, w_value, w_out)
    total = pl.pallas_call(
        reduce_kernel,
        out_shape=shape(4, 2, 1024, 256),
        in_specs=[VM],
        out_specs=VM,
        scratch_shapes=[
            pltpu.VMEM((4, 1024, 256), BF),
            pltpu.VMEM((4, 1024, 256), BF),
            pltpu.VMEM((4, 3, 256, 256), BF),
            pltpu.VMEM((4, 256, 256), BF),
            pltpu.VMEM((4, 3, 64, 256), BF),
            pltpu.VMEM((4, 64, 256), BF),
            pltpu.VMEM((4, 3, 16, 256), BF),
            DMA((2, 4)),
            DMA((2, 4)),
            DMA((3, 4, 3)),
            DMA((3, 4, 3)),
            DMA((3, 4, 3)),
            DMA((3, 4, 3)),
        ],
        compiler_params=params(2, 40),
        name="total",
    )(wg)
    weights = [jnp.concatenate([total[m, 0], total[m, 1]], axis=1).astype(F32) for m in range(3)]
    last = total[3].reshape(4, 512, 256).transpose(1, 0, 2).reshape(512, 1024).astype(F32)
    return (mixed[None], gin[None], *weights, last)


def solution(mesh):
    placed = (P("dp", "seq", None), P("dp", None), P(), P(), P(), P(), P("dp", "seq", None))
    return jax.shard_map(
        local,
        mesh=mesh,
        in_specs=placed,
        out_specs=(P("dp", "seq", None), P("dp", "seq", None), P(), P(), P(), P()),
        check_vma=False,
    )
```

time: 754 us -> 192 us (0.25); the launches traced: 742 us -> 192 us
  waiting for transfers between devices: 300 us -> 0 us
  local copies, waits for them, and re-layouts: 193 us -> 16.6 us
  Pallas kernels: 0 us -> 170 us
  starting transfers between devices: 121 us -> 0 us
  matrix products: 65 us -> 0 us
  other arithmetic: 48.3 us -> 4.38 us
  between operations: 15.3 us -> 0.75 us
    psum x1 -> x0, waiting for transfers between devices: 179 us -> none  [local(): lax.psum(weight_terms[0].astype(jnp.bfloat16), ('dp', 'seq'))]
    pallas_call x0 -> x4, Pallas kernels: none -> 170 us  [the longest x1 54.1 us: local(): pl.pallas_call(reduce_kernel, out_shape=shape(4, 2, 1024, 256), in_specs=...]
    ppermute x32 -> x0, starting transfers between devices: 101 us -> none  [shifted(): return lax.ppermute(block, axis, route)]
    ppermute x32 -> x0, waiting for transfers between devices: 100 us -> none  [shifted(): return lax.ppermute(block, axis, route)]
    dot_general x24 -> x0, matrix products: 65 us -> none  [the longest x19 53.9 us: product(): return jnp.einsum(form, left, right, preferred_element_type=jnp.float32)]
    unnamed x142 -> x26, local copies, waits for them, and re-layouts: 76.9 us -> 14.8 us
    another operation x31 -> x0, local copies, waits for them, and re-layouts: 40.5 us -> none  [the longest x9 20.7 us: bar_block(): jnp.stack(key_parts, 1)]
    all_to_all x2 -> x0, waiting for transfers between devices: 21.3 us -> none  [the longest x1 21.3 us: sent_to_all(): lax.all_to_all(jnp.broadcast_to(shard[None], (count, *shard.shape)), axis...]
  transfers between devices with their start and end apart: 35 -> 0, of which waited for: 10 -> 0; matrix products, arithmetic and copies ran while one was open for 22% -> 0% of each run, Pallas kernels for 0% -> 0%
where the time goes in v1:
time: 192 us
  Pallas kernels  170 us (89%)
  local copies, waits for them, and re-layouts  16.6 us (9%)
  other arithmetic  4.38 us (2%)
    pallas_call x1, Pallas kernels, local(): pl.pallas_call(reduce_kernel, out_shape=shape(4, 2, 1024, 256), in_specs=...  54.1 us
    pallas_call x1, Pallas kernels, local(): pl.pallas_call(spread_kernel, out_shape=(shape(6144, 256), shape(2048, 25...  43.7 us
    pallas_call x1, Pallas kernels, local(): pl.pallas_call(back_kernel, out_shape=(shape(512, 1024), shape(512, 1024)...  39.4 us
    pallas_call x1, Pallas kernels, local(): pl.pallas_call(attend_kernel, out_shape=(shape(2048, 256), shape(6144, 25...  32.7 us
    unnamed x26, local copies, waits for them, and re-layouts  14.8 us
    convert_element_type x2, other arithmetic, local(): jnp.concatenate([total[m, 0], total[m, 1]], axis=1).astype(F32)  4.21 us

profile of v1, /device:TPU:1, one launch (start us, length us, event | category | flops | bytes accessed | tf_op | source)
XLA Modules:
  0.0 191.8 jit_solution(10589936634984640066)
XLA Ops:
  0.6 0.0 copy-start.2
  0.6 1.2 copy-done.2
  1.9 1.2 copy-done.4
  3.1 1.2 copy-done.6
  4.3 1.2 copy-done.7
  5.5 1.2 copy-done.8
  6.8 1.2 copy-done.9
  8.0 0.7 copy-done.10
  8.6 43.7 %spread.1 = (bf16[6144,256]{1,0:T(8,128)(2,1)S(1)}, bf16[2048,256]{1,0:T(8,128)(2,1)S(1)}, bf16[8,16,256]{2,1,0:T(8,128)(2,1)S(1)}) custom-call(s32[1,128]{1,0:T(1,128)S(1)} %copy-done.10, bf16[512,1024]{1,0:T(8,128)(2,1)S(1)} %bitcast.23, bf16[512,1024]{1,0:T(8,128)(2,1)S(1)} %bitcast.25, bf16[1024,512]{1,0:T(8,128)(2,1)S(1)} %copy-done.6, ...), custom_call_target="tpu_custom_call" | custom-call | tf_op jit(solution)/shard_map/spread/pallas_call | solution.py:557
  52.4 0.0 copy-start.5
  52.4 0.0 copy-start.11
  52.4 32.7 %attend.1 = (bf16[2048,256]{1,0:T(8,128)(2,1)S(1)}, f32[6144,256]{1,0:T(8,128)S(1)}, f32[128,256]{1,0:T(8,128)S(1)}) custom-call(s32[1,128]{1,0:T(1,128)S(1)} %copy-done.10, bf16[6144,256]{1,0:T(8,128)(2,1)S(1)} %get-tuple-element.15.kv, bf16[2048,256]{1,0:T(8,128)(2,1)S(1)} %get-tuple-element.16.qg, bf16[128,256]{1,0:T(8,128)(2,1)S(1)} %bitcast.29), custom_call_target="tpu_custom_call" | custom-call | tf_op jit(solution)/shard_map/attend/pallas_call | solution.py:572
  85.1 2.7 %copy-done = f32[6144,256]{1,0:T(8,128)} copy-done((f32[6144,256]{1,0:T(8,128)}, f32[6144,256]{1,0:T(8,128)S(1)}, u32[]{:S(2)}) %copy-start) | copy-done | bytes 6291480
  87.8 39.4 %back.1 = (bf16[512,1024]{1,0:T(8,128)(2,1)S(1)}, bf16[512,1024]{1,0:T(8,128)(2,1)S(1)}, bf16[4,2,1024,256]{3,2,1,0:T(8,128)(2,1)}) custom-call(s32[1,128]{1,0:T(1,128)S(1)} %copy-done.11, f32[6144,256]{1,0:T(8,128)} %copy-done, f32[128,256]{1,0:T(8,128)S(1)} %get-tuple-element.19.gsum, bf16[2048,256]{1,0:T(8,128)(2,1)S(1)} %get-tuple-element.20.cg, ...), custom_call_target="tpu_custom_call" | custom-call | tf_op jit(solution)/shard_map/back/pallas_call | solution.py:587
  127.3 2.2 %copy-done.1 = bf16[4,2,1024,256]{3,2,1,0:T(8,128)(2,1)S(1)} copy-done((bf16[4,2,1024,256]{3,2,1,0:T(8,128)(2,1)S(1)}, bf16[4,2,1024,256]{3,2,1,0:T(8,128)(2,1)}, u32[]{:S(2)}) %copy-start.1) | copy-done | bytes 4194328
  129.4 54.1 %total.1 = bf16[4,2,1024,256]{3,2,1,0:T(8,128)(2,1)S(1)} custom-call(bf16[4,2,1024,256]{3,2,1,0:T(8,128)(2,1)S(1)} %copy-done.1), custom_call_target="tpu_custom_call" | custom-call | tf_op jit(solution)/shard_map/total/pallas_call | solution.py:605
  183.6 0.1 slice.27
  183.6 0.2 slice_bitcast_fusion.1
  183.8 0.2 convert_bitcast_fusion
  184.0 1.6 copy.14
  185.6 1.6 maximum_convert_fusion.2
  187.2 2.6 %maximum_convert_fusion = (f32[1024,512]{1,0:T(8,128)}, f32[1024,512]{1,0:T(8,128)}) fusion(bf16[1024,256]{1,0:T(8,128)(2,1)S(1)} %get-tuple-element.28, bf16[1024,256]{1,0:T(8,128)(2,1)S(1)} %get-tuple-element.29, bf16[1024,256]{1,0:T(8,128)(2,1)S(1)} %get-tuple-element.26, bf16[1024,256]{1,0:T(8,128)(2,1)S(1)} %get-tuple-element.27), kind=kLoop, calls=%fused_computation.1 | loop fusion | flops 4194304 | bytes 6291456 | tf_op jit(solution)/shard_map/convert_element_type | solution.py:628
  189.8 1.0 copy.17
  190.8 1.0 copy.18
  (12 shorter events, 0.0 us)
Async XLA Ops:
  0.6 1.2 copy-start.2
  1.9 1.2 copy-start.4
  3.1 1.2 copy-start.6
  4.3 1.2 copy-start.7
  5.5 1.2 copy-start.8
  6.8 1.2 copy-start.9
  8.0 0.7 copy-start.10
  52.4 35.4 %copy-start.3 = (bf16[1,512,1024]{2,1,0:T(8,128)(2,1)S(1)}, bf16[1,512,1024]{2,1,0:T(8,128)(2,1)}, u32[]{:S(2)}) copy-start(bf16[1,512,1024]{2,1,0:T(8,128)(2,1)} %param.7) | copy-start | bytes 3145732
  52.4 35.4 %copy-start.5 = (bf16[1,512,1024]{2,1,0:T(8,128)(2,1)S(1)}, bf16[1,512,1024]{2,1,0:T(8,128)(2,1)}, u32[]{:S(2)}) copy-start(bf16[1,512,1024]{2,1,0:T(8,128)(2,1)} %param.13) | copy-start | bytes 3145732
  52.4 35.4 %copy-start.11 = (s32[1,128]{1,0:T(1,128)S(1)}, s32[1,128]{1,0:T(1,128)}, u32[]{:S(2)}) copy-start(s32[1,128]{1,0:T(1,128)} %lens.5) | copy-start | bytes 1540
  85.1 2.7 %copy-start = (f32[6144,256]{1,0:T(8,128)}, f32[6144,256]{1,0:T(8,128)S(1)}, u32[]{:S(2)}) copy-start(f32[6144,256]{1,0:T(8,128)S(1)} %get-tuple-element.18.gkv) | copy-start | bytes 18874372
  127.2 2.2 %copy-start.1 = (bf16[4,2,1024,256]{3,2,1,0:T(8,128)(2,1)S(1)}, bf16[4,2,1024,256]{3,2,1,0:T(8,128)(2,1)}, u32[]{:S(2)}) copy-start(bf16[4,2,1024,256]{3,2,1,0:T(8,128)(2,1)} %get-tuple-element.23.wg) | copy-start | bytes 12582916

commit v2 on v1

v2 whole, which is shorter than its diff:
```python
import functools
import math

import jax
import jax.numpy as jnp
from jax import lax
from jax.experimental import pallas as pl
from jax.experimental.pallas import tpu as pltpu
from jax.sharding import PartitionSpec as P

MESH = pl.DeviceIdType.MESH
BF = jnp.bfloat16
F32 = jnp.float32
HEADS = 4
TILE = 128
OFFSETS = (0, 1, 2, 4, 8, 12, 16, 24, 32)
SCALE = 1.0 / math.sqrt(128.0)
LOG2E = 1.4426950408889634
NEG = -1e30
NT = (((1,), (1,)), ((), ()))
TN = (((0,), (0,)), ((), ()))
OWN = 32 * TILE
MIB = 1024 * 1024


def place():
    s = lax.axis_index("seq")
    return lax.axis_index("dp"), lax.div(s, 8), lax.rem(lax.div(s, 2), 4), lax.rem(s, 2)


def device(y, x, z, c):
    return (y, (x * 4 + z) * 2 + c)


def turn(a, d):
    return lax.rem(a + d, 4)


def remote(src, dst, send, recv, to):
    return pltpu.make_async_remote_copy(
        src_ref=src, dst_ref=dst, send_sem=send, recv_sem=recv, device_id=to, device_id_type=MESH
    )


def greet(partners):
    barrier = pltpu.get_barrier_semaphore()
    for to in partners:
        pl.semaphore_signal(barrier, inc=1, device_id=to, device_id_type=MESH)
    pl.semaphore_wait(barrier, len(partners))


def all_partners(y, x, z, c):
    found = [device(y, x, z, 1 - c)]
    for d in (1, 2, 3):
        found.append(device(turn(y, d), x, z, c))
        for core in (0, 1):
            found.append(device(y, turn(x, d), z, core))
            found.append(device(y, x, turn(z, d), core))
    return found


def rows_of(start, count):
    return pl.ds(pl.multiple_of(start, TILE), count)


def whole_kernel(
    lens, tok_in, wk_in, wv_in, wq_in, cot_in, wo_in, mixed, gin, out,
    tok, cot, wq, wk, wv, wo,
    kv, qg, summ, kvs, qgs, sums,
    kvt, gt, pair, pairt, sc, dsp, gkv, gsum, cg,
    sx, rx, sh, rh, gss, gsr, own, ret_kv, ret_cg, flat,
    wg, got0, w0, got1, w1, got2, w2, got3,
    s_in, s_kv, r_kv, s_qg, r_qg, s_h, r_h, s_x, r_x, s_s, r_s,
    s_bkv, r_bkv, s_cg, r_cg, s_bh, r_bh, s_bx, r_bx, s_gs, r_gs,
    s0, r0, s1, r1, s2, r2,
):
    y, x, z, c = place()
    loads = []
    for n, (a, b) in enumerate(
        ((tok_in, tok), (wk_in, wk), (wv_in, wv), (wq_in, wq), (cot_in, cot), (wo_in, wo))
    ):
        copy = pltpu.make_async_copy(a, b, s_in.at[n])
        copy.start()
        loads.append(copy)
    greet(all_partners(y, x, z, c))
    other = device(y, x, z, 1 - c)
    home = lax.div(z, 2)
    at_home = c == home
    slot = lax.rem(z, 2) * 2 + c
    group = 2 * x + c

    def project(src, w, dst, lane):
        def half(i, carry):
            rows = rows_of(i * 256, 256)
            got = jnp.dot(src[rows, :], w[...], preferred_element_type=F32)
            for h in range(HEADS):
                dst[h, rows, lane : lane + TILE] = got[:, h * TILE : (h + 1) * TILE].astype(BF)
            return carry

        lax.fori_loop(0, 2, half, 0)

    def exchange(staged, landing, base, send, recv):
        spot = rows_of(base + slot * 512, 512)
        copies = []
        near = remote(staged.at[z], landing.at[spot], send.at[0], recv.at[slot], other)

        @pl.when(at_home)
        def _():
            landing[spot, :] = staged[z]

        @pl.when(jnp.logical_not(at_home))
        def _():
            near.start()

        for d in (1, 3, 2):
            h = turn(z, d)
            copy = remote(staged.at[h], landing.at[spot], send.at[d], recv.at[slot], device(y, x, h, home))
            copy.start()
            copies.append(copy)
        return copies, near

    def settle_out(copies, near):
        for copy in copies:
            copy.wait_send()

        @pl.when(jnp.logical_not(at_home))
        def _():
            near.wait_send()

    def arrived(staged, landing, base, send, recv, i):
        mine = jnp.logical_and(z == 2 * c + lax.div(i, 2), c == lax.rem(i, 2))

        @pl.when(jnp.logical_not(mine))
        def _():
            remote(
                staged.at[0], landing.at[rows_of(base + i * 512, 512)], send.at[0], recv.at[i], other
            ).wait_recv()

    for n in range(3):
        loads[n].wait()
    project(tok, wk, kvs, 0)
    project(tok, wv, kvs, TILE)
    kv_sent = exchange(kvs, kv, OWN, s_kv, r_kv)
    for n in range(3, 6):
        loads[n].wait()
    project(tok, wq, qgs, 0)
    first_own = ((x * 4 + z) * 2 + c) * 4

    def grads(i, carry):
        rows = rows_of(i * TILE, TILE)
        got = lax.dot_general(cot[rows, :], wo[...], NT, preferred_element_type=F32)
        live = lax.broadcasted_iota(jnp.int32, (TILE, 512), 0) < lens[0, first_own + i]
        got = jnp.where(live, got, 0.0).astype(BF)
        for h in range(HEADS):
            qgs[h, rows, TILE : 2 * TILE] = got[:, h * TILE : (h + 1) * TILE]
        return carry

    lax.fori_loop(0, 4, grads, 0)
    qg_sent = exchange(qgs, qg, 0, s_qg, r_qg)

    ahead = device(y, turn(x, 1), z, c)
    behind = device(y, turn(x, 3), z, c)

    def halo_copy(i):
        return remote(
            kv.at[rows_of(OWN + i * 512, 512)], kv.at[rows_of(i * 512, 512)], s_h.at[i], r_h.at[i], ahead
        )

    def across_copy(start, i):
        return remote(
            kv.at[rows_of(start + i * 512, 512)],
            kv.at[rows_of(2048 + i * 512, 512)],
            s_x.at[i],
            r_x.at[i],
            other,
        )

    order = [lax.rem(lax.rem(z, 2) * 2 + k, 4) for k in range(4)]
    for i in order:
        arrived(kvs, kv, OWN, s_kv, r_kv, i)
        halo_copy(i).start()

        @pl.when(c == 0)
        def _():
            across_copy(OWN, i).start()

    def summary(i, carry):
        rows = rows_of(OWN + i * TILE, TILE)
        length = lens[0, group * 16 + i]
        live = lax.broadcasted_iota(jnp.int32, (TILE, 256), 0) < length
        total = jnp.sum(jnp.where(live, kv[rows, :].astype(F32), 0.0), axis=0, keepdims=True)
        sums[pl.ds(i, 1), :] = total / jnp.full((1, 256), length, jnp.int32).astype(F32)
        return carry

    lax.fori_loop(0, 16, summary, 0)
    summ[group] = sums[...].astype(BF)
    sum_copies = []
    pairs_of = [(d, cc) for d in range(4) for cc in (0, 1) if (d, cc) != (0, 0)]
    for d, cc in pairs_of:
        n = d * 2 + cc
        core = lax.rem(c + cc, 2)
        copy = remote(summ.at[group], summ.at[group], s_s.at[n], r_s.at[n], device(y, turn(x, d), z, core))
        copy.start()
        sum_copies.append(copy)

    def prepare(b, carry):
        rows = rows_of(b * TILE, TILE)
        kvt[:, rows] = jnp.transpose(kv[rows, :])
        return carry

    def clear(b, carry):
        gkv[rows_of(b * TILE, TILE), :] = jnp.zeros((TILE, 256), F32)
        return carry

    lax.fori_loop(0, 48, clear, 0)
    gsum[...] = jnp.zeros_like(gsum)
    for u in range(UNROLL):
        pair[u] = jnp.zeros((256, 256), BF)
        pairt[u] = jnp.zeros((256, 256), BF)
    lax.fori_loop(32, 48, prepare, 0)
    for k in range(4):
        i = lax.rem(lax.rem(z, 2) * 2 + k, 4)
        halo_copy(i).wait_recv()

        @pl.when(c == 1)
        def _():
            across_copy(0, i).start()

    lax.fori_loop(0, 16, prepare, 0)
    for i in range(4):
        across_copy(0, i).wait()
        halo_copy(i).wait_send()
        arrived(qgs, qg, 0, s_qg, r_qg, i)
    lax.fori_loop(16, 32, prepare, 0)
    for copy in sum_copies:
        copy.wait()
    kvt[:, 48 * TILE : 49 * TILE] = jnp.transpose(summ[...].reshape(TILE, 256))
    settle_out(*kv_sent)
    settle_out(*qg_sent)

    key_slot = lax.broadcasted_iota(jnp.int32, (TILE, TILE), 0)
    query_slot = lax.broadcasted_iota(jnp.int32, (TILE, TILE), 1)
    count = len(OFFSETS)

    def bar(it, carry):
        ids = [it * UNROLL + u for u in range(UNROLL)]
        tops, scales, deltas = [], [], []
        for u, qb in enumerate(ids):
            rows = rows_of(qb * TILE, TILE)
            pair[u, 0:TILE, 0:TILE] = qg[rows, 0:TILE]
            pair[u, TILE:, TILE:] = qg[rows, TILE:]
            pairt[u, 0:TILE, 0:TILE] = jnp.transpose(qg[rows, 0:TILE])
            pairt[u, TILE:, TILE:] = jnp.transpose(qg[rows, TILE:])
            both = pairt[u]
            this = 16 * group + qb
            top = None
            for j in range(count + 1):
                here = slice(j * TILE, (j + 1) * TILE)
                if j < count:
                    spot = rows_of((32 + qb - OFFSETS[j]) * TILE, TILE)
                    bar_id = this - OFFSETS[j]
                    length = jnp.where(bar_id >= 0, lens[0, jnp.maximum(bar_id, 0)], 0)
                    source = kv[spot, :]
                    gt[u, :, here] = kvt[:, spot]
                    ok = key_slot < length
                    if j == 0:
                        ok = jnp.logical_and(ok, key_slot <= query_slot)
                else:
                    source = summ[...].reshape(TILE, 256)
                    gt[u, :, here] = kvt[:, 48 * TILE : 49 * TILE]
                    distance = this - key_slot
                    ok = distance >= 1
                    for o in OFFSETS[1:]:
                        ok = jnp.logical_and(ok, distance != o)
                got = jnp.dot(source, both, preferred_element_type=F32)
                score = jnp.where(ok, got[:, :TILE] * (SCALE * LOG2E), NEG)
                sc[u, here, :TILE] = score
                sc[u, here, TILE:] = got[:, TILE:]
                high = jnp.max(score, axis=0, keepdims=True)
                top = high if top is None else jnp.maximum(top, high)
            tops.append(top)
        for u in range(UNROLL):
            total = jnp.zeros((1, TILE), F32)
            weighted = jnp.zeros((1, TILE), F32)
            for j in range(count + 1):
                here = slice(j * TILE, (j + 1) * TILE)
                e = jnp.exp2(sc[u, here, :TILE] - tops[u])
                sc[u, here, :TILE] = e
                total = total + jnp.sum(e, axis=0, keepdims=True)
                weighted = weighted + jnp.sum(e * sc[u, here, TILE:], axis=0, keepdims=True)
            scales.append(1.0 / total)
            deltas.append(weighted * scales[u])
        for u, qb in enumerate(ids):
            rows = rows_of(qb * TILE, TILE)
            both = pair[u]
            for j in range(count + 1):
                here = slice(j * TILE, (j + 1) * TILE)
                p = sc[u, here, :TILE] * scales[u]
                ds = (p * (sc[u, here, TILE:] - deltas[u])).astype(BF)
                block = jnp.concatenate([ds, p.astype(BF)], axis=1)
                dsp[u, here, :] = block
                got = jnp.dot(block, both, preferred_element_type=F32)
                if j < count:
                    spot = rows_of((32 + qb - OFFSETS[j]) * TILE, TILE)
                    gkv[spot, :] += got
                else:
                    gsum[...] += got
            both_out = jnp.dot(gt[u], dsp[u], preferred_element_type=F32)
            cg[rows, 0:TILE] = jnp.transpose(both_out[:TILE, :TILE] * SCALE).astype(BF)
            context = jnp.transpose(both_out[TILE:, TILE:])
            cg[rows, TILE:] = jnp.where(key_slot < lens[0, 16 * group + qb], context, 0.0).astype(BF)
        return carry

    def owner(i):
        to_z = 2 * c + lax.div(i, 2)
        core = lax.rem(i, 2)
        mine = jnp.logical_and(z == to_z, c == core)
        return device(y, x, to_z, core), mine

    def give_back(src, landing, send, recv, i):
        to, mine = owner(i)
        rows = rows_of(i * 512, 512)

        @pl.when(mine)
        def _():
            landing[z] = src[rows, :]

        @pl.when(jnp.logical_not(mine))
        def _():
            remote(src.at[rows], landing.at[z], send.at[i], recv.at[z], to).start()

    def settle(src, landing, send, recv):
        for i in range(4):
            to, mine = owner(i)

            @pl.when(jnp.logical_not(mine))
            def _():
                remote(src.at[pl.ds(i * 512, 512)], landing.at[z], send.at[i], recv.at[z], to).wait_send()

    def returned(src, landing, send, recv):
        for h in range(HEADS):
            mine = jnp.logical_and(z == h, at_home)

            @pl.when(jnp.logical_not(mine))
            def _():
                remote(src.at[pl.ds(0, 512)], landing.at[h], send.at[0], recv.at[h], other).wait_recv()

    def crossing(i):
        rows = rows_of(i * 512, 512)
        return remote(sx.at[rows], rx.at[rows], s_bx.at[i], r_bx.at[i], other)

    def cross(i):
        sx[rows_of(i * 512, 512), :] = gkv[rows_of(2048 + i * 512, 512), :].astype(BF)
        crossing(i).start()

    def halo_back(i):
        rows = rows_of(i * 512, 512)
        return remote(sh.at[rows], rh.at[rows], s_bh.at[i], r_bh.at[i], behind)

    def chunk(i, carry):
        lax.fori_loop(i * (4 // UNROLL), (i + 1) * (4 // UNROLL), bar, 0)

        @pl.when(c == 0)
        def _():
            rows = rows_of(i * 512, 512)
            sh[rows, :] = gkv[rows, :].astype(BF)
            halo_back(i).start()

        @pl.when(i >= 2)
        def _():
            cross(i - 2)
            cross(i)

        give_back(cg, ret_cg, s_cg, r_cg, i)
        return carry

    lax.fori_loop(0, 4, chunk, 0)
    gss[...] = gsum[...].astype(BF).reshape(8, 16, 256)
    gsr[group] = gss[group]
    back_copies = []
    for d, cc in pairs_of:
        n = d * 2 + cc
        to_x, core = turn(x, d), lax.rem(c + cc, 2)
        copy = remote(
            gss.at[to_x * 2 + core], gsr.at[group], s_gs.at[n], r_gs.at[n], device(y, to_x, z, core)
        )
        copy.start()
        back_copies.append(copy)
    turns = (0, 2, 1, 3)
    for i in turns:
        crossing(i).wait_recv()

        @pl.when(c == 1)
        def _():
            rows = pl.ds(i * 512, 512)
            sh[rows, :] = (gkv[rows, :] + rx[rows, :].astype(F32)).astype(BF)
            halo_back(i).start()

    def flatten(src, lane, n):
        for h in range(HEADS):
            flat[n, :, h * TILE : (h + 1) * TILE] = src[h, :, lane : lane + TILE]

    where = {"y": y, "x": x, "z": z}
    levels = ((w0, got1, 256), (w1, got2, 64), (w2, got3, 16))
    pending = [None] * 4
    started = []
    last = []

    def along(axis, d):
        at = dict(where)
        at[axis] = turn(where[axis], d)
        return device(at["y"], at["x"], at["z"], c)

    def core_half(m):
        return remote(wg.at[m, 1 - c], got0.at[m], s0.at[0, m], r0.at[0, m], other)

    def send_level(m, level):
        src, got, size = levels[level]
        copies = []
        axis = ORDERS[m][level]
        for d in (1, 2, 3):
            piece = pl.ds(pl.multiple_of(turn(where[axis], d) * size, 16), size)
            copy = remote(
                src.at[m, piece], got.at[m, d - 1], s1.at[level, m, d - 1], r1.at[level, m, d - 1], along(axis, d)
            )
            copy.start()
            copies.append(copy)
        pending[m] = copies
        started.extend(copies)

    def place_rows(m, level):
        a, b, d = (where[axis] for axis in ORDERS[m])
        start = a * 256
        if level >= 1:
            start = start + b * 64
        if level >= 2:
            start = start + d * 16
        return pl.ds(pl.multiple_of(start, 16), levels[level][2])

    half = pl.ds(pl.multiple_of(c * 256, 256), 256)

    def give(m, level):
        block = out.at[m, place_rows(m, level), half]
        copies = []
        for d in (1, 2, 3):
            copy = remote(
                block, block, s2.at[level, m, d - 1], r2.at[level, m, d - 1], along(ORDERS[m][level], d)
            )
            copy.start()
            copies.append(copy)
        pending[m] = copies
        started.extend(copies)

    def settled(m):
        for copy in pending[m]:
            copy.wait_recv()

    def begin(m):
        core_half(m).wait_recv()

        def add(i, carry):
            rows = rows_of(i * 256, 256)
            w0[m, rows, :] = (wg[m, c, rows, :].astype(F32) + got0[m, rows, :].astype(F32)).astype(BF)
            return carry

        lax.fori_loop(0, 4, add, 0)
        send_level(m, 0)

    def advance(m, level):
        src, got, size = levels[level]
        settled(m)
        mine = pl.ds(pl.multiple_of(where[ORDERS[m][level]] * size, 16), size)
        total = src[m, mine, :].astype(F32)
        for n in range(3):
            total = total + got[m, n].astype(F32)
        if level < 2:
            levels[level + 1][0][m] = total.astype(BF)
            send_level(m, level + 1)
        else:
            out[m, place_rows(m, 2), half] = total.astype(BF)
            give(m, 2)

    def finish(m):
        settled(m)
        copy = remote(out.at[m, :, half], out.at[m, :, half], s0.at[1, m], r0.at[1, m], other)
        copy.start()
        last.append(copy)

    def weight_grad(n, m):
        def part(i, carry):
            cols = rows_of(i * 256, 256)
            got = lax.dot_general(tok[:, cols], flat[n], TN, preferred_element_type=F32).astype(BF)
            wg[m, 0, cols, :] = got[:, :256]
            wg[m, 1, cols, :] = got[:, 256:]
            return carry

        lax.fori_loop(0, 4, part, 0)
        core_half(m).start()

    returned(cg, ret_cg, s_cg, r_cg)
    flatten(ret_cg, 0, 0)
    weight_grad(0, 0)
    flatten(ret_cg, TILE, 3)

    def out_grad(i, carry):
        cols = rows_of(i * 256, 256)
        got = lax.dot_general(flat[3], cot[:, cols], TN, preferred_element_type=F32).astype(BF)
        wg[3, lax.rem(i, 2), rows_of(lax.div(i, 2) * 512, 512), :] = got
        return carry

    lax.fori_loop(0, 4, out_grad, 0)
    core_half(3).start()
    begin(0)
    begin(3)

    for copy in back_copies:
        copy.wait()
    coarse = gsr[0].astype(F32)
    for n in range(1, 8):
        coarse = coarse + gsr[n].astype(F32)
    lane = lax.broadcasted_iota(jnp.int32, (1, 256), 1)
    factor = jnp.where(lane < TILE, SCALE, 1.0)
    for i in turns:
        halo_back(i).wait_recv()
        for b in range(4 * i, 4 * i + 4):
            rows = pl.ds(b * TILE, TILE)
            length = lens[0, group * 16 + b]
            live = lax.broadcasted_iota(jnp.int32, (TILE, 256), 0) < length
            share = coarse[b : b + 1, :] * (1.0 / jnp.full((1, 256), length, jnp.int32).astype(F32))
            extra = jnp.where(c == 0, rx[rows, :].astype(F32), 0.0)
            total = gkv[pl.ds(OWN + b * TILE, TILE), :] + rh[rows, :].astype(F32) + extra
            own[rows, :] = ((total + jnp.where(live, share, 0.0)) * factor).astype(BF)
        give_back(own, ret_kv, s_bkv, r_bkv, i)

    def mix(i, carry):
        rows = rows_of(i * 256, 256)
        mixed[rows, :] = jnp.dot(flat[3, rows, :], wo[...], preferred_element_type=F32).astype(BF)
        return carry

    lax.fori_loop(0, 2, mix, 0)
    advance(0, 0)
    advance(3, 0)
    returned(own, ret_kv, s_bkv, r_bkv)
    flatten(ret_kv, 0, 1)
    weight_grad(1, 1)
    flatten(ret_kv, TILE, 2)
    weight_grad(2, 2)
    begin(1)
    begin(2)
    advance(0, 1)
    advance(3, 1)
    advance(0, 2)
    advance(3, 2)

    def back(i, carry):
        rows = rows_of(i * 256, 256)
        total = lax.dot_general(flat[0, rows, :], wq[...], NT, preferred_element_type=F32)
        total = total + lax.dot_general(flat[1, rows, :], wk[...], NT, preferred_element_type=F32)
        total = total + lax.dot_general(flat[2, rows, :], wv[...], NT, preferred_element_type=F32)
        gin[rows, :] = total.astype(BF)
        return carry

    lax.fori_loop(0, 2, back, 0)
    for m in (0, 3):
        settled(m)
        give(m, 1)
    for m in (1, 2):
        advance(m, 0)
    for m in (0, 3):
        settled(m)
        give(m, 0)
    for level in (1, 2):
        for m in (1, 2):
            advance(m, level)
    for level in (1, 0):
        for m in (1, 2):
            settled(m)
            give(m, level)
    for m in (0, 3, 1, 2):
        finish(m)
    for copy in last:
        copy.wait()
    for m in range(4):
        core_half(m).wait_send()
        crossing(m).wait_send()
        halo_back(m).wait_send()
    for copy in started:
        copy.wait_send()
    settle(cg, ret_cg, s_cg, r_cg)
    settle(own, ret_kv, s_bkv, r_bkv)


ORDERS = ("yxz", "xzy", "zyx", "yzx")
UNROLL = 2

HB = pl.BlockSpec(memory_space=pl.ANY)
VM = pl.BlockSpec(memory_space=pltpu.VMEM)
SM = pl.BlockSpec(memory_space=pltpu.SMEM)
DMA = pltpu.SemaphoreType.DMA


def shape(*dims, kind=BF):
    return jax.ShapeDtypeStruct(dims, kind)


def local(tokens, lengths, w_query, w_key, w_value, w_out, cotangent):
    vm = pltpu.VMEM
    slabs = lambda n: [vm((2048, 256), BF)] * n
    heads = lambda n: [vm((4, 512, 256), BF)] * n
    mixed, gin, total = pl.pallas_call(
        whole_kernel,
        out_shape=(shape(512, 1024), shape(512, 1024), shape(4, 1024, 512)),
        in_specs=[SM] + [HB] * 6,
        out_specs=(VM, VM, VM),
        scratch_shapes=[vm((512, 1024), BF)] * 2
        + [vm((1024, 512), BF)] * 3
        + [vm((512, 1024), BF), vm((6144, 256), BF)]
        + slabs(1)
        + [vm((8, 16, 256), BF)]
        + heads(2)
        + [vm((16, 256), F32)]
        + [
            vm((256, 49 * TILE), BF),
            vm((UNROLL, 256, 10 * TILE), BF),
            vm((UNROLL, 256, 256), BF),
            vm((UNROLL, 256, 256), BF),
            vm((UNROLL, 10 * TILE, 256), F32),
            vm((UNROLL, 10 * TILE, 256), BF),
            vm((6144, 256), F32),
            vm((128, 256), F32),
        ]
        + slabs(5)
        + [vm((8, 16, 256), BF)] * 2
        + slabs(1)
        + heads(2)
        + [
            vm((4, 512, 512), BF),
            vm((4, 2, 1024, 256), BF),
            vm((4, 1024, 256), BF),
            vm((4, 1024, 256), BF),
            vm((4, 3, 256, 256), BF),
            vm((4, 256, 256), BF),
            vm((4, 3, 64, 256), BF),
            vm((4, 64, 256), BF),
            vm((4, 3, 16, 256), BF),
        ]
        + [DMA((6,))]
        + [DMA((4,))] * 8
        + [DMA((8,))] * 2
        + [DMA((4,))] * 8
        + [DMA((8,))] * 2
        + [DMA((2, 4))] * 2
        + [DMA((3, 4, 3))] * 4,
        compiler_params=pltpu.CompilerParams(
            collective_id=0, has_side_effects=True, vmem_limit_bytes=62 * MIB
        ),
        name="whole",
    )(lengths, tokens[0], w_key, w_value, w_query, cotangent[0], w_out)
    weights = [total[m].astype(F32) for m in range(3)]
    last = jnp.concatenate([total[3, :512], total[3, 512:]], axis=1).astype(F32)
    return (mixed[None], gin[None], *weights, last)


def solution(mesh):
    placed = (P("dp", "seq", None), P("dp", None), P(), P(), P(), P(), P("dp", "seq", None))
    return jax.shard_map(
        local,
        mesh=mesh,
        in_specs=placed,
        out_specs=(P("dp", "seq", None), P("dp", "seq", None), P(), P(), P(), P()),
        check_vma=False,
    )
```

time: 192 us -> 151 us (0.79)
  Pallas kernels: 170 us -> 141 us
  local copies, waits for them, and re-layouts: 16.6 us -> 3.22 us
  other arithmetic: 4.38 us -> 6.43 us
    pallas_call x4 -> x1, Pallas kernels: 170 us -> 141 us  [local(): pl.pallas_call(whole_kernel, out_shape=(shape(512, 1024), shape(512, 1024...]
    unnamed x26 -> x6, local copies, waits for them, and re-layouts: 14.8 us -> 1.95 us
    convert_element_type x2, other arithmetic: 4.21 us -> 6.43 us  [the longest x1 4.85 us: local(): weights = [total[m].astype(F32) for m in range(3)]]
where the time goes in v2:
time: 151 us
  Pallas kernels  141 us (93%)
  other arithmetic  6.43 us (4%)
  local copies, waits for them, and re-layouts  3.22 us (2%)
    pallas_call x1, Pallas kernels, local(): pl.pallas_call(whole_kernel, out_shape=(shape(512, 1024), shape(512, 1024...  141 us
    convert_element_type x1, other arithmetic, local(): weights = [total[m].astype(F32) for m in range(3)]  4.85 us

profile of v2, /device:TPU:1, one launch (start us, length us, event | category | flops | bytes accessed | tf_op | source)
XLA Modules:
  0.0 150.9 jit_solution(13938533519450285480)
XLA Ops:
  0.6 140.5 %whole.1 = (bf16[512,1024]{1,0:T(8,128)(2,1)}, bf16[512,1024]{1,0:T(8,128)(2,1)}, bf16[4,1024,512]{2,1,0:T(8,128)(2,1)}) custom-call(s32[1,128]{1,0:T(1,128)} %lens.1, bf16[512,1024]{1,0:T(8,128)(2,1)} %bitcast.17, bf16[1024,512]{1,0:T(8,128)(2,1)} %wk_in.1, bf16[1024,512]{1,0:T(8,128)(2,1)} %wv_in.1, bf16[1024,512]{1,0:T(8,128)(2,1)} %wq_in.1, ...), custom_call_target="tpu_custom_call" | custom-call | tf_op jit(solution)/shard_map/whole/pallas_call | solution.py:610
  141.2 4.8 %bitcast_convert_fusion = (f32[1024,512]{1,0:T(8,128)}, f32[1024,512]{1,0:T(8,128)}, f32[1024,512]{1,0:T(8,128)}) fusion(bf16[4,1024,512]{2,1,0:T(8,128)(2,1)} %get-tuple-element.11), kind=kLoop, calls=%fused_computation.1 | loop fusion | flops 1572864 | bytes 9437184 | tf_op jit(solution)/shard_map/convert_element_type | solution.py:659
  146.0 1.3 slice_bitcast_fusion.1
  147.3 0.0 copy-start.1
  147.3 0.0 copy-start
  147.3 1.6 %maximum_convert_fusion = f32[512,1024]{1,0:T(8,128)} fusion(bf16[512,512]{1,0:T(8,128)(2,1)S(1)} %get-tuple-element.13, bf16[512,512]{1,0:T(8,128)(2,1)S(1)} %get-tuple-element.12), kind=kLoop, calls=%fused_computation | loop fusion | flops 2097152 | bytes 3145728 | tf_op jit(solution)/shard_map/convert_element_type | solution.py:660
  148.9 0.0 copy-done.1
  148.9 1.0 copy.15
  149.9 0.0 copy-done
  149.9 1.0 copy.16
Async XLA Ops:
  147.3 1.6 %copy-start.1 = (bf16[512,1024]{1,0:T(8,128)(2,1)S(1)}, bf16[512,1024]{1,0:T(8,128)(2,1)}, u32[]{:S(2)}) copy-start(bf16[512,1024]{1,0:T(8,128)(2,1)} %get-tuple-element.9) | copy-start | bytes 3145732
  147.3 2.6 %copy-start = (bf16[512,1024]{1,0:T(8,128)(2,1)S(1)}, bf16[512,1024]{1,0:T(8,128)(2,1)}, u32[]{:S(2)}) copy-start(bf16[512,1024]{1,0:T(8,128)(2,1)} %get-tuple-element.10) | copy-start | bytes 3145732

commit v3 on v2

--- a/solution.py
+++ b/solution.py
@@ -69,7 +69,7 @@
     kv, qg, summ, kvs, qgs, sums,
     kvt, gt, pair, pairt, sc, dsp, gkv, gsum, cg,
     sx, rx, sh, rh, gss, gsr, own, ret_kv, ret_cg, flat,
-    wg, got0, w0, got1, w1, got2, w2, got3,
+    wg, got0, w0, got1, w1, got2, got3,
     s_in, s_kv, r_kv, s_qg, r_qg, s_h, r_h, s_x, r_x, s_s, r_s,
     s_bkv, r_bkv, s_cg, r_cg, s_bh, r_bh, s_bx, r_bx, s_gs, r_gs,
     s0, r0, s1, r1, s2, r2,
@@ -401,7 +401,7 @@
             flat[n, :, h * TILE : (h + 1) * TILE] = src[h, :, lane : lane + TILE]
 
     where = {"y": y, "x": x, "z": z}
-    levels = ((w0, got1, 256), (w1, got2, 64), (w2, got3, 16))
+    levels = ((w0, got1, 256), (w1, got2, 64))
     pending = [None] * 4
     started = []
     last = []
@@ -429,12 +429,9 @@
         started.extend(copies)
 
     def place_rows(m, level):
-        a, b, d = (where[axis] for axis in ORDERS[m])
-        start = a * 256
-        if level >= 1:
-            start = start + b * 64
-        if level >= 2:
-            start = start + d * 16
+        start = where[ORDERS[m][0]] * 256
+        if level == 1:
+            start = start + where[ORDERS[m][1]] * 64
         return pl.ds(pl.multiple_of(start, 16), levels[level][2])
 
     half = pl.ds(pl.multiple_of(c * 256, 256), 256)
@@ -467,18 +464,33 @@
         send_level(m, 0)
 
     def advance(m, level):
+        settled(m)
+        if level == 2:
+            total = got3[m, 0].astype(F32)
+            for n in range(1, 4):
+                total = total + got3[m, n].astype(F32)
+            out[m, place_rows(m, 1), half] = total.astype(BF)
+            give(m, 1)
+            return
         src, got, size = levels[level]
-        settled(m)
         mine = pl.ds(pl.multiple_of(where[ORDERS[m][level]] * size, 16), size)
         total = src[m, mine, :].astype(F32)
         for n in range(3):
             total = total + got[m, n].astype(F32)
-        if level < 2:
-            levels[level + 1][0][m] = total.astype(BF)
-            send_level(m, level + 1)
+        if level == 0:
+            w1[m] = total.astype(BF)
+            send_level(m, 1)
         else:
-            out[m, place_rows(m, 2), half] = total.astype(BF)
-            give(m, 2)
+            axis = ORDERS[m][2]
+            got3[m, where[axis]] = total.astype(BF)
+            block = got3.at[m, where[axis]]
+            copies = []
+            for d in (1, 2, 3):
+                copy = remote(block, block, s1.at[2, m, d - 1], r1.at[2, m, d - 1], along(axis, d))
+                copy.start()
+                copies.append(copy)
+            pending[m] = copies
+            started.extend(copies)
 
     def finish(m):
         settled(m)
@@ -538,8 +550,9 @@
         return carry
 
     lax.fori_loop(0, 2, mix, 0)
-    advance(0, 0)
-    advance(3, 0)
+    for level in range(3):
+        advance(0, level)
+        advance(3, level)
     returned(own, ret_kv, s_bkv, r_bkv)
     flatten(ret_kv, 0, 1)
     weight_grad(1, 1)
@@ -547,10 +560,9 @@
     weight_grad(2, 2)
     begin(1)
     begin(2)
-    advance(0, 1)
-    advance(3, 1)
-    advance(0, 2)
-    advance(3, 2)
+    for m in (0, 3):
+        settled(m)
+        give(m, 0)
 
     def back(i, carry):
         rows = rows_of(i * 256, 256)
@@ -561,21 +573,12 @@
         return carry
 
     lax.fori_loop(0, 2, back, 0)
-    for m in (0, 3):
-        settled(m)
-        give(m, 1)
+    for level in range(3):
+        advance(1, level)
+        advance(2, level)
     for m in (1, 2):
-        advance(m, 0)
-    for m in (0, 3):
         settled(m)
         give(m, 0)
-    for level in (1, 2):
-        for m in (1, 2):
-            advance(m, level)
-    for level in (1, 0):
-        for m in (1, 2):
-            settled(m)
-            give(m, level)
     for m in (0, 3, 1, 2):
         finish(m)
     for copy in last:
@@ -588,6 +591,15 @@
         copy.wait_send()
     settle(cg, ret_cg, s_cg, r_cg)
     settle(own, ret_kv, s_bkv, r_bkv)
+
+
+def hand_over(mixed, gin, a, b, c, low, high, mixed_out, gin_out, a_out, b_out, c_out, d_out):
+    mixed_out[...] = mixed[...]
+    gin_out[...] = gin[...]
+    for src, dst in ((a, a_out), (b, b_out), (c, c_out)):
+        dst[...] = src[0].astype(F32)
+    d_out[:, :512] = low[0].astype(F32)
+    d_out[:, 512:] = high[0].astype(F32)
 
 
 ORDERS = ("yxz", "xzy", "zyx", "yzx")
@@ -641,8 +653,7 @@
             vm((4, 3, 256, 256), BF),
             vm((4, 256, 256), BF),
             vm((4, 3, 64, 256), BF),
-            vm((4, 64, 256), BF),
-            vm((4, 3, 16, 256), BF),
+            vm((4, 4, 64, 256), BF),
         ]
         + [DMA((6,))]
         + [DMA((4,))] * 8
@@ -650,15 +661,30 @@
         + [DMA((4,))] * 8
         + [DMA((8,))] * 2
         + [DMA((2, 4))] * 2
-        + [DMA((3, 4, 3))] * 4,
+        + [DMA((3, 4, 3))] * 2
+        + [DMA((2, 4, 3))] * 2,
         compiler_params=pltpu.CompilerParams(
             collective_id=0, has_side_effects=True, vmem_limit_bytes=62 * MIB
         ),
         name="whole",
     )(lengths, tokens[0], w_key, w_value, w_query, cotangent[0], w_out)
-    weights = [total[m].astype(F32) for m in range(3)]
-    last = jnp.concatenate([total[3, :512], total[3, 512:]], axis=1).astype(F32)
-    return (mixed[None], gin[None], *weights, last)
+    block = pl.BlockSpec
+    mixed, gin, *weights = pl.pallas_call(
+        hand_over,
+        grid=(8,),
+        out_shape=(shape(512, 1024), shape(512, 1024))
+        + (shape(1024, 512, kind=F32),) * 3
+        + (shape(512, 1024, kind=F32),),
+        in_specs=[block((64, 1024), lambda i: (i, 0))] * 2
+        + [block((1, 128, 512), lambda i, m=m: (m, i, 0)) for m in range(3)]
+        + [block((1, 64, 512), lambda i, n=n: (3, n + i, 0)) for n in (0, 8)],
+        out_specs=[block((64, 1024), lambda i: (i, 0))] * 2
+        + [block((128, 512), lambda i: (i, 0))] * 3
+        + [block((64, 1024), lambda i: (i, 0))],
+        compiler_params=pltpu.CompilerParams(vmem_limit_bytes=40 * MIB),
+        name="hand_over",
+    )(mixed, gin, total, total, total, total, total)
+    return (mixed[None], gin[None], *weights)
 
 
 def solution(mesh):

time: 151 us -> 145 us (0.960)
  other arithmetic: 6.43 us -> 0 us
    convert_element_type x2 -> x0, other arithmetic: 6.43 us -> none  [the longest x1 4.85 us: local(): weights = [total[m].astype(F32) for m in range(3)]]
    pallas_call x1, Pallas kernels: 141 us -> 135 us  [local(): pl.pallas_call(whole_kernel, out_shape=(shape(512, 1024), shape(512, 1024...]
    pallas_call x0 -> x1, Pallas kernels: none -> 4.8 us  [local(): pl.pallas_call(hand_over, grid=(8,), out_shape=(shape(512, 1024), shape(5...]
    unnamed x6, local copies, waits for them, and re-layouts: 1.95 us -> 4.63 us
where the time goes in v3:
time: 145 us
  Pallas kernels  140 us (97%)
  local copies, waits for them, and re-layouts  4.63 us (3%)
    pallas_call x1, Pallas kernels, local(): pl.pallas_call(whole_kernel, out_shape=(shape(512, 1024), shape(512, 1024...  135 us
    pallas_call x1, Pallas kernels, local(): pl.pallas_call(hand_over, grid=(8,), out_shape=(shape(512, 1024), shape(5...  4.8 us
    unnamed x6, local copies, waits for them, and re-layouts  4.63 us

profile of v3, /device:TPU:1, one launch (start us, length us, event | category | flops | bytes accessed | tf_op | source)
XLA Modules:
  0.0 145.1 jit_solution(3439778046245353809)
XLA Ops:
  0.6 135.0 %whole.1 = (bf16[512,1024]{1,0:T(8,128)(2,1)}, bf16[512,1024]{1,0:T(8,128)(2,1)}, bf16[4,1024,512]{2,1,0:T(8,128)(2,1)}) custom-call(s32[1,128]{1,0:T(1,128)} %lens.1, bf16[512,1024]{1,0:T(8,128)(2,1)} %bitcast.4, bf16[1024,512]{1,0:T(8,128)(2,1)} %wk_in.1, bf16[1024,512]{1,0:T(8,128)(2,1)} %wv_in.1, bf16[1024,512]{1,0:T(8,128)(2,1)} %wq_in.1, ...), custom_call_target="tpu_custom_call" | custom-call | tf_op jit(solution)/shard_map/whole/pallas_call | solution.py:622
  135.6 0.0 copy-start
  135.6 2.2 %copy-done = bf16[4,1024,512]{2,1,0:T(8,128)(2,1)S(1)} copy-done((bf16[4,1024,512]{2,1,0:T(8,128)(2,1)S(1)}, bf16[4,1024,512]{2,1,0:T(8,128)(2,1)}, u32[]{:S(2)}) %copy-start) | copy-done | bytes 4194328
  137.8 0.0 copy-start.1
  137.8 1.2 copy-done.1
  139.0 0.0 copy-start.2
  139.0 1.2 copy-done.2
  140.3 4.8 %hand_over.1 = (bf16[512,1024]{1,0:T(8,128)(2,1)}, bf16[512,1024]{1,0:T(8,128)(2,1)}, f32[1024,512]{1,0:T(8,128)}, f32[1024,512]{1,0:T(8,128)}, f32[1024,512]{1,0:T(8,128)}, /*index=5*/f32[512,1024]{1,0:T(8,128)}) custom-call(bf16[512,1024]{1,0:T(8,128)(2,1)S(1)} %copy-done.1, bf16[512,1024]{1,0:T(8,128)(2,1)S(1)} %copy-done.2, ...), custom_call_target="tpu_custom_call" | custom-call | tf_op jit(solution)/shard_map/hand_over/pallas_call | solution.py:672
Async XLA Ops:
  135.6 2.2 %copy-start = (bf16[4,1024,512]{2,1,0:T(8,128)(2,1)S(1)}, bf16[4,1024,512]{2,1,0:T(8,128)(2,1)}, u32[]{:S(2)}) copy-start(bf16[4,1024,512]{2,1,0:T(8,128)(2,1)} %get-tuple-element.17.a.b.c.low.high) | copy-start | bytes 12582916
  137.8 1.2 copy-start.1
  139.0 1.2 copy-start.2

commit v4 on v3

--- a/solution.py
+++ b/solution.py
@@ -40,13 +40,6 @@
     return pltpu.make_async_remote_copy(
         src_ref=src, dst_ref=dst, send_sem=send, recv_sem=recv, device_id=to, device_id_type=MESH
     )
-
-
-def greet(partners):
-    barrier = pltpu.get_barrier_semaphore()
-    for to in partners:
-        pl.semaphore_signal(barrier, inc=1, device_id=to, device_id_type=MESH)
-    pl.semaphore_wait(barrier, len(partners))
 
 
 def all_partners(y, x, z, c):
@@ -82,7 +75,10 @@
         copy = pltpu.make_async_copy(a, b, s_in.at[n])
         copy.start()
         loads.append(copy)
-    greet(all_partners(y, x, z, c))
+    partners = all_partners(y, x, z, c)
+    barrier = pltpu.get_barrier_semaphore()
+    for to in partners:
+        pl.semaphore_signal(barrier, inc=1, device_id=to, device_id_type=MESH)
     other = device(y, x, z, 1 - c)
     home = lax.div(z, 2)
     at_home = c == home
@@ -140,6 +136,7 @@
         loads[n].wait()
     project(tok, wk, kvs, 0)
     project(tok, wv, kvs, TILE)
+    pl.semaphore_wait(barrier, len(partners))
     kv_sent = exchange(kvs, kv, OWN, s_kv, r_kv)
     for n in range(3, 6):
         loads[n].wait()
@@ -156,8 +153,6 @@
         return carry
 
     lax.fori_loop(0, 4, grads, 0)
-    qg_sent = exchange(qgs, qg, 0, s_qg, r_qg)
-
     ahead = device(y, turn(x, 1), z, c)
     behind = device(y, turn(x, 3), z, c)
 
@@ -183,6 +178,8 @@
         @pl.when(c == 0)
         def _():
             across_copy(OWN, i).start()
+
+    qg_sent = exchange(qgs, qg, 0, s_qg, r_qg)
 
     def summary(i, carry):
         rows = rows_of(OWN + i * TILE, TILE)
@@ -550,7 +547,7 @@
         return carry
 
     lax.fori_loop(0, 2, mix, 0)
-    for level in range(3):
+    for level in range(2):
         advance(0, level)
         advance(3, level)
     returned(own, ret_kv, s_bkv, r_bkv)
@@ -560,9 +557,8 @@
     weight_grad(2, 2)
     begin(1)
     begin(2)
-    for m in (0, 3):
-        settled(m)
-        give(m, 0)
+    advance(0, 2)
+    advance(3, 2)
 
     def back(i, carry):
         rows = rows_of(i * 256, 256)
@@ -573,6 +569,9 @@
         return carry
 
     lax.fori_loop(0, 2, back, 0)
+    for m in (0, 3):
+        settled(m)
+        give(m, 0)
     for level in range(3):
         advance(1, level)
         advance(2, level)
@@ -603,7 +602,7 @@
 
 
 ORDERS = ("yxz", "xzy", "zyx", "yzx")
-UNROLL = 2
+UNROLL = 4
 
 HB = pl.BlockSpec(memory_space=pl.ANY)
 VM = pl.BlockSpec(memory_space=pltpu.VMEM)
@@ -681,7 +680,7 @@
         out_specs=[block((64, 1024), lambda i: (i, 0))] * 2
         + [block((128, 512), lambda i: (i, 0))] * 3
         + [block((64, 1024), lambda i: (i, 0))],
-        compiler_params=pltpu.CompilerParams(vmem_limit_bytes=40 * MIB),
+        compiler_params=pltpu.CompilerParams(vmem_limit_bytes=62 * MIB),
         name="hand_over",
     )(mixed, gin, total, total, total, total, total)
     return (mixed[None], gin[None], *weights)

time: 145 us -> 147 us (1.014)
  Pallas kernels: 140 us -> 146 us
  local copies, waits for them, and re-layouts: 4.63 us -> 0 us
    unnamed x6 -> x0, local copies, waits for them, and re-layouts: 4.63 us -> none
    pallas_call x1, Pallas kernels: 4.8 us -> 8.42 us  [local(): pl.pallas_call(hand_over, grid=(8,), out_shape=(shape(512, 1024), shape(5...]
    pallas_call x1, Pallas kernels: 135 us -> 137 us  [local(): pl.pallas_call(whole_kernel, out_shape=(shape(512, 1024), shape(512, 1024...]
where the time goes in v4:
time: 147 us; the launch traced here: 146 us
  Pallas kernels  146 us (99%)
    pallas_call x1, Pallas kernels, local(): pl.pallas_call(whole_kernel, out_shape=(shape(512, 1024), shape(512, 1024...  137 us
    pallas_call x1, Pallas kernels, local(): pl.pallas_call(hand_over, grid=(8,), out_shape=(shape(512, 1024), shape(5...  8.42 us

profile of v4, /device:TPU:1, one launch (start us, length us, event | category | flops | bytes accessed | tf_op | source)
XLA Modules:
  0.0 146.2 jit_solution(8710934970632539817)
XLA Ops:
  0.6 137.2 %whole.1 = (bf16[512,1024]{1,0:T(8,128)(2,1)}, bf16[512,1024]{1,0:T(8,128)(2,1)}, bf16[4,1024,512]{2,1,0:T(8,128)(2,1)}) custom-call(s32[1,128]{1,0:T(1,128)} %lens.1, bf16[512,1024]{1,0:T(8,128)(2,1)} %bitcast.4, bf16[1024,512]{1,0:T(8,128)(2,1)} %wk_in.1, bf16[1024,512]{1,0:T(8,128)(2,1)} %wv_in.1, bf16[1024,512]{1,0:T(8,128)(2,1)} %wq_in.1, ...), custom_call_target="tpu_custom_call" | custom-call | tf_op jit(solution)/shard_map/whole/pallas_call | solution.py:621
  137.8 8.4 %hand_over.1 = (bf16[512,1024]{1,0:T(8,128)(2,1)}, bf16[512,1024]{1,0:T(8,128)(2,1)}, f32[1024,512]{1,0:T(8,128)}, f32[1024,512]{1,0:T(8,128)}, f32[1024,512]{1,0:T(8,128)}, /*index=5*/f32[512,1024]{1,0:T(8,128)}) custom-call(bf16[512,1024]{1,0:T(8,128)(2,1)} %get-tuple-element.15.mixed, bf16[512,1024]{1,0:T(8,128)(2,1)} %get-tuple-element.16.gin, ...), custom_call_target="tpu_custom_call" | custom-call | tf_op jit(solution)/shard_map/hand_over/pallas_call | solution.py:671

commit v5 on v4

--- a/solution.py
+++ b/solution.py
@@ -58,10 +58,10 @@
 
 def whole_kernel(
     lens, tok_in, wk_in, wv_in, wq_in, cot_in, wo_in, mixed, gin, out,
-    tok, cot, wq, wk, wv, wo,
+    tok, tokt, cot, wq, wk, wv, wo,
     kv, qg, summ, kvs, qgs, sums,
     kvt, gt, pair, pairt, sc, dsp, gkv, gsum, cg,
-    sx, rx, sh, rh, gss, gsr, own, ret_kv, ret_cg, flat,
+    rx, rh, gss, gsr, ret_kv, ret_cg, flat,
     wg, got0, w0, got1, w1, got2, got3,
     s_in, s_kv, r_kv, s_qg, r_qg, s_h, r_h, s_x, r_x, s_s, r_s,
     s_bkv, r_bkv, s_cg, r_cg, s_bh, r_bh, s_bx, r_bx, s_gs, r_gs,
@@ -111,7 +111,8 @@
         for d in (1, 3, 2):
             h = turn(z, d)
             copy = remote(staged.at[h], landing.at[spot], send.at[d], recv.at[slot], device(y, x, h, home))
-            copy.start()
+            if d != 2:
+                copy.start()
             copies.append(copy)
         return copies, near
 
@@ -153,6 +154,8 @@
         return carry
 
     lax.fori_loop(0, 4, grads, 0)
+    kv_sent[0][2].start()
+
     ahead = device(y, turn(x, 1), z, c)
     behind = device(y, turn(x, 3), z, c)
 
@@ -170,7 +173,8 @@
             other,
         )
 
-    order = [lax.rem(lax.rem(z, 2) * 2 + k, 4) for k in range(4)]
+    nearest = lax.rem(z + jnp.where(at_home, 0, 1), 2) * 2
+    order = [lax.rem(nearest + k, 4) for k in range(4)]
     for i in order:
         arrived(kvs, kv, OWN, s_kv, r_kv, i)
         halo_copy(i).start()
@@ -180,6 +184,7 @@
             across_copy(OWN, i).start()
 
     qg_sent = exchange(qgs, qg, 0, s_qg, r_qg)
+    qg_sent[0][2].start()
 
     def summary(i, carry):
         rows = rows_of(OWN + i * TILE, TILE)
@@ -215,8 +220,14 @@
         pair[u] = jnp.zeros((256, 256), BF)
         pairt[u] = jnp.zeros((256, 256), BF)
     lax.fori_loop(32, 48, prepare, 0)
-    for k in range(4):
-        i = lax.rem(lax.rem(z, 2) * 2 + k, 4)
+
+    def turned(i, carry):
+        cols = rows_of(i * TILE, TILE)
+        tokt[cols, :] = jnp.transpose(tok[:, cols])
+        return carry
+
+    lax.fori_loop(0, 8, turned, 0)
+    for i in order:
         halo_copy(i).wait_recv()
 
         @pl.when(c == 1)
@@ -344,15 +355,15 @@
 
     def crossing(i):
         rows = rows_of(i * 512, 512)
-        return remote(sx.at[rows], rx.at[rows], s_bx.at[i], r_bx.at[i], other)
+        return remote(kvs.at[i], rx.at[rows], s_bx.at[i], r_bx.at[i], other)
 
     def cross(i):
-        sx[rows_of(i * 512, 512), :] = gkv[rows_of(2048 + i * 512, 512), :].astype(BF)
+        kvs[i] = gkv[rows_of(2048 + i * 512, 512), :].astype(BF)
         crossing(i).start()
 
     def halo_back(i):
         rows = rows_of(i * 512, 512)
-        return remote(sh.at[rows], rh.at[rows], s_bh.at[i], r_bh.at[i], behind)
+        return remote(qgs.at[i], rh.at[rows], s_bh.at[i], r_bh.at[i], behind)
 
     def chunk(i, carry):
         lax.fori_loop(i * (4 // UNROLL), (i + 1) * (4 // UNROLL), bar, 0)
@@ -360,7 +371,7 @@
         @pl.when(c == 0)
         def _():
             rows = rows_of(i * 512, 512)
-            sh[rows, :] = gkv[rows, :].astype(BF)
+            qgs[i] = gkv[rows, :].astype(BF)
             halo_back(i).start()
 
         @pl.when(i >= 2)
@@ -390,7 +401,7 @@
         @pl.when(c == 1)
         def _():
             rows = pl.ds(i * 512, 512)
-            sh[rows, :] = (gkv[rows, :] + rx[rows, :].astype(F32)).astype(BF)
+            qgs[i] = (gkv[rows, :] + rx[rows, :].astype(F32)).astype(BF)
             halo_back(i).start()
 
     def flatten(src, lane, n):
@@ -498,7 +509,7 @@
     def weight_grad(n, m):
         def part(i, carry):
             cols = rows_of(i * 256, 256)
-            got = lax.dot_general(tok[:, cols], flat[n], TN, preferred_element_type=F32).astype(BF)
+            got = jnp.dot(tokt[cols, :], flat[n], preferred_element_type=F32).astype(BF)
             wg[m, 0, cols, :] = got[:, :256]
             wg[m, 1, cols, :] = got[:, 256:]
             return carry
@@ -538,8 +549,8 @@
             share = coarse[b : b + 1, :] * (1.0 / jnp.full((1, 256), length, jnp.int32).astype(F32))
             extra = jnp.where(c == 0, rx[rows, :].astype(F32), 0.0)
             total = gkv[pl.ds(OWN + b * TILE, TILE), :] + rh[rows, :].astype(F32) + extra
-            own[rows, :] = ((total + jnp.where(live, share, 0.0)) * factor).astype(BF)
-        give_back(own, ret_kv, s_bkv, r_bkv, i)
+            qg[rows, :] = ((total + jnp.where(live, share, 0.0)) * factor).astype(BF)
+        give_back(qg, ret_kv, s_bkv, r_bkv, i)
 
     def mix(i, carry):
         rows = rows_of(i * 256, 256)
@@ -547,18 +558,17 @@
         return carry
 
     lax.fori_loop(0, 2, mix, 0)
-    for level in range(2):
-        advance(0, level)
-        advance(3, level)
-    returned(own, ret_kv, s_bkv, r_bkv)
+    advance(0, 0)
+    advance(3, 0)
+    returned(qg, ret_kv, s_bkv, r_bkv)
     flatten(ret_kv, 0, 1)
     weight_grad(1, 1)
     flatten(ret_kv, TILE, 2)
     weight_grad(2, 2)
     begin(1)
     begin(2)
-    advance(0, 2)
-    advance(3, 2)
+    advance(0, 1)
+    advance(3, 1)
 
     def back(i, carry):
         rows = rows_of(i * 256, 256)
@@ -569,10 +579,14 @@
         return carry
 
     lax.fori_loop(0, 2, back, 0)
+    advance(0, 2)
+    advance(3, 2)
+    advance(1, 0)
+    advance(2, 0)
     for m in (0, 3):
         settled(m)
         give(m, 0)
-    for level in range(3):
+    for level in (1, 2):
         advance(1, level)
         advance(2, level)
     for m in (1, 2):
@@ -589,16 +603,32 @@
     for copy in started:
         copy.wait_send()
     settle(cg, ret_cg, s_cg, r_cg)
-    settle(own, ret_kv, s_bkv, r_bkv)
-
-
-def hand_over(mixed, gin, a, b, c, low, high, mixed_out, gin_out, a_out, b_out, c_out, d_out):
-    mixed_out[...] = mixed[...]
-    gin_out[...] = gin[...]
-    for src, dst in ((a, a_out), (b, b_out), (c, c_out)):
-        dst[...] = src[0].astype(F32)
-    d_out[:, :512] = low[0].astype(F32)
-    d_out[:, 512:] = high[0].astype(F32)
+    settle(qg, ret_kv, s_bkv, r_bkv)
+
+
+def hand_over(mixed, gin, total, *refs):
+    mixed_out, gin_out, outs = refs[0], refs[1], refs[2:6]
+    narrow, wide, s_in, s_out, s_pass = refs[6:]
+    passed = [
+        pltpu.make_async_copy(mixed, mixed_out, s_pass.at[0]),
+        pltpu.make_async_copy(gin, gin_out, s_pass.at[1]),
+    ]
+    loads, stores = [], []
+    for n in range(8):
+        piece = pl.ds((n % 2) * 512, 512)
+        loads.append(pltpu.make_async_copy(total.at[n // 2, piece], narrow.at[n], s_in.at[n]))
+    for copy in loads + passed:
+        copy.start()
+    for n in range(8):
+        loads[n].wait()
+        wide[n] = narrow[n].astype(F32)
+        piece = pl.ds((n % 2) * 512, 512)
+        to = outs[3].at[:, piece] if n >= 6 else outs[n // 2].at[piece]
+        copy = pltpu.make_async_copy(wide.at[n], to, s_out.at[n])
+        copy.start()
+        stores.append(copy)
+    for copy in stores + passed:
+        copy.wait()
 
 
 ORDERS = ("yxz", "xzy", "zyx", "yzx")
@@ -623,7 +653,7 @@
         out_shape=(shape(512, 1024), shape(512, 1024), shape(4, 1024, 512)),
         in_specs=[SM] + [HB] * 6,
         out_specs=(VM, VM, VM),
-        scratch_shapes=[vm((512, 1024), BF)] * 2
+        scratch_shapes=[vm((512, 1024), BF), vm((1024, 512), BF), vm((512, 1024), BF)]
         + [vm((1024, 512), BF)] * 3
         + [vm((512, 1024), BF), vm((6144, 256), BF)]
         + slabs(1)
@@ -640,9 +670,8 @@
             vm((6144, 256), F32),
             vm((128, 256), F32),
         ]
-        + slabs(5)
+        + slabs(3)
         + [vm((8, 16, 256), BF)] * 2
-        + slabs(1)
         + heads(2)
         + [
             vm((4, 512, 512), BF),
@@ -667,22 +696,17 @@
         ),
         name="whole",
     )(lengths, tokens[0], w_key, w_value, w_query, cotangent[0], w_out)
-    block = pl.BlockSpec
     mixed, gin, *weights = pl.pallas_call(
         hand_over,
-        grid=(8,),
         out_shape=(shape(512, 1024), shape(512, 1024))
         + (shape(1024, 512, kind=F32),) * 3
         + (shape(512, 1024, kind=F32),),
-        in_specs=[block((64, 1024), lambda i: (i, 0))] * 2
-        + [block((1, 128, 512), lambda i, m=m: (m, i, 0)) for m in range(3)]
-        + [block((1, 64, 512), lambda i, n=n: (3, n + i, 0)) for n in (0, 8)],
-        out_specs=[block((64, 1024), lambda i: (i, 0))] * 2
-        + [block((128, 512), lambda i: (i, 0))] * 3
-        + [block((64, 1024), lambda i: (i, 0))],
+        in_specs=[HB] * 3,
+        out_specs=(HB,) * 6,
+        scratch_shapes=[vm((8, 512, 512), BF), vm((8, 512, 512), F32), DMA((8,)), DMA((8,)), DMA((2,))],
         compiler_params=pltpu.CompilerParams(vmem_limit_bytes=62 * MIB),
         name="hand_over",
-    )(mixed, gin, total, total, total, total, total)
+    )(mixed, gin, total)
     return (mixed[None], gin[None], *weights)
 
 

time: 147 us -> 198 us (1.35)
  Pallas kernels: 146 us -> 198 us
    pallas_call x1, Pallas kernels: 8.42 us -> 64.8 us  [local(): pl.pallas_call(hand_over, out_shape=(shape(512, 1024), shape(512, 1024))...]
    pallas_call x1, Pallas kernels: 137 us -> 133 us  [local(): pl.pallas_call(whole_kernel, out_shape=(shape(512, 1024), shape(512, 1024...]
where the time goes in v5:
time: 198 us
  Pallas kernels  198 us (100%)
    pallas_call x1, Pallas kernels, local(): pl.pallas_call(whole_kernel, out_shape=(shape(512, 1024), shape(512, 1024...  133 us
    pallas_call x1, Pallas kernels, local(): pl.pallas_call(hand_over, out_shape=(shape(512, 1024), shape(512, 1024))...  64.8 us

profile of v5, /device:TPU:1, one launch (start us, length us, event | category | flops | bytes accessed | tf_op | source)
XLA Modules:
  0.0 198.2 jit_solution(16225442773114565238)
XLA Ops:
  0.6 132.8 %whole.1 = (bf16[512,1024]{1,0:T(8,128)(2,1)}, bf16[512,1024]{1,0:T(8,128)(2,1)}, bf16[4,1024,512]{2,1,0:T(8,128)(2,1)}) custom-call(s32[1,128]{1,0:T(1,128)} %lens.1, bf16[512,1024]{1,0:T(8,128)(2,1)} %bitcast.4, bf16[1024,512]{1,0:T(8,128)(2,1)} %wk_in.1, bf16[1024,512]{1,0:T(8,128)(2,1)} %wv_in.1, bf16[1024,512]{1,0:T(8,128)(2,1)} %wq_in.1, ...), custom_call_target="tpu_custom_call" | custom-call | tf_op jit(solution)/shard_map/whole/pallas_call | solution.py:651
  133.4 64.8 %hand_over.1 = (bf16[512,1024]{1,0:T(8,128)(2,1)}, bf16[512,1024]{1,0:T(8,128)(2,1)}, f32[1024,512]{1,0:T(8,128)}, f32[1024,512]{1,0:T(8,128)}, f32[1024,512]{1,0:T(8,128)}, /*index=5*/f32[512,1024]{1,0:T(8,128)}) custom-call(bf16[512,1024]{1,0:T(8,128)(2,1)} %get-tuple-element.15.mixed, bf16[512,1024]{1,0:T(8,128)(2,1)} %get-tuple-element.16.gin, ...), custom_call_target="tpu_custom_call" | custom-call | tf_op jit(solution)/shard_map/hand_over/pallas_call | solution.py:699

commit v6 on v5

--- a/solution.py
+++ b/solution.py
@@ -581,18 +581,20 @@
     lax.fori_loop(0, 2, back, 0)
     advance(0, 2)
     advance(3, 2)
-    advance(1, 0)
-    advance(2, 0)
-    for m in (0, 3):
-        settled(m)
-        give(m, 0)
-    for level in (1, 2):
+    settled(0)
+    give(0, 0)
+    for level in (0, 1):
         advance(1, level)
         advance(2, level)
+    settled(3)
+    give(3, 0)
+    advance(1, 2)
+    advance(2, 2)
+    finish(0)
     for m in (1, 2):
         settled(m)
         give(m, 0)
-    for m in (0, 3, 1, 2):
+    for m in (3, 1, 2):
         finish(m)
     for copy in last:
         copy.wait()
@@ -608,30 +610,35 @@
 
 def hand_over(mixed, gin, total, *refs):
     mixed_out, gin_out, outs = refs[0], refs[1], refs[2:6]
-    narrow, wide, s_in, s_out, s_pass = refs[6:]
+    narrow, wide, s_in, s_out, kept, s_kept, s_pass = refs[6:]
+    halves = [pl.ds(0, 512), pl.ds(512, 512)]
+    held = [
+        pltpu.make_async_copy(src, kept.at[n], s_kept.at[n]) for n, src in enumerate((mixed, gin))
+    ]
     passed = [
-        pltpu.make_async_copy(mixed, mixed_out, s_pass.at[0]),
-        pltpu.make_async_copy(gin, gin_out, s_pass.at[1]),
+        pltpu.make_async_copy(kept.at[n], dst, s_pass.at[n])
+        for n, dst in enumerate((mixed_out, gin_out))
     ]
-    loads, stores = [], []
-    for n in range(8):
-        piece = pl.ds((n % 2) * 512, 512)
-        loads.append(pltpu.make_async_copy(total.at[n // 2, piece], narrow.at[n], s_in.at[n]))
-    for copy in loads + passed:
+    loads = [
+        pltpu.make_async_copy(total.at[n // 2, halves[n % 2]], narrow.at[n], s_in.at[n]) for n in range(8)
+    ]
+    for copy in loads + held:
         copy.start()
+    stores = []
     for n in range(8):
         loads[n].wait()
         wide[n] = narrow[n].astype(F32)
-        piece = pl.ds((n % 2) * 512, 512)
-        to = outs[3].at[:, piece] if n >= 6 else outs[n // 2].at[piece]
-        copy = pltpu.make_async_copy(wide.at[n], to, s_out.at[n])
-        copy.start()
-        stores.append(copy)
+        to = outs[3].at[:, halves[n % 2]] if n >= 6 else outs[n // 2].at[halves[n % 2]]
+        stores.append(pltpu.make_async_copy(wide.at[n], to, s_out.at[n]))
+        stores[n].start()
+    for n in range(2):
+        held[n].wait()
+        passed[n].start()
     for copy in stores + passed:
         copy.wait()
 
 
-ORDERS = ("yxz", "xzy", "zyx", "yzx")
+ORDERS = ("yxz", "xzy", "zxy", "yzx")
 UNROLL = 4
 
 HB = pl.BlockSpec(memory_space=pl.ANY)
@@ -703,7 +710,8 @@
         + (shape(512, 1024, kind=F32),),
         in_specs=[HB] * 3,
         out_specs=(HB,) * 6,
-        scratch_shapes=[vm((8, 512, 512), BF), vm((8, 512, 512), F32), DMA((8,)), DMA((8,)), DMA((2,))],
+        scratch_shapes=[vm((8, 512, 512), BF), vm((8, 512, 512), F32), DMA((8,)), DMA((8,))]
+        + [vm((2, 512, 1024), BF), DMA((2,)), DMA((2,))],
         compiler_params=pltpu.CompilerParams(vmem_limit_bytes=62 * MIB),
         name="hand_over",
     )(mixed, gin, total)

time: 198 us -> 135 us (0.68)
  Pallas kernels: 198 us -> 135 us
    pallas_call x1, Pallas kernels: 64.8 us -> 5.81 us  [local(): pl.pallas_call(hand_over, out_shape=(shape(512, 1024), shape(512, 1024))...]
    pallas_call x1, Pallas kernels: 133 us -> 129 us  [local(): pl.pallas_call(whole_kernel, out_shape=(shape(512, 1024), shape(512, 1024...]
where the time goes in v6:
time: 135 us
  Pallas kernels  135 us (100%)
    pallas_call x1, Pallas kernels, local(): pl.pallas_call(whole_kernel, out_shape=(shape(512, 1024), shape(512, 1024...  129 us
    pallas_call x1, Pallas kernels, local(): pl.pallas_call(hand_over, out_shape=(shape(512, 1024), shape(512, 1024))...  5.81 us

profile of v6, /device:TPU:1, one launch (start us, length us, event | category | flops | bytes accessed | tf_op | source)
XLA Modules:
  0.0 135.4 jit_solution(3513401879213465647)
XLA Ops:
  0.6 128.9 %whole.1 = (bf16[512,1024]{1,0:T(8,128)(2,1)}, bf16[512,1024]{1,0:T(8,128)(2,1)}, bf16[4,1024,512]{2,1,0:T(8,128)(2,1)}) custom-call(s32[1,128]{1,0:T(1,128)} %lens.1, bf16[512,1024]{1,0:T(8,128)(2,1)} %bitcast.4, bf16[1024,512]{1,0:T(8,128)(2,1)} %wk_in.1, bf16[1024,512]{1,0:T(8,128)(2,1)} %wv_in.1, bf16[1024,512]{1,0:T(8,128)(2,1)} %wq_in.1, ...), custom_call_target="tpu_custom_call" | custom-call | tf_op jit(solution)/shard_map/whole/pallas_call | solution.py:658
  129.6 5.8 %hand_over.1 = (bf16[512,1024]{1,0:T(8,128)(2,1)}, bf16[512,1024]{1,0:T(8,128)(2,1)}, f32[1024,512]{1,0:T(8,128)}, f32[1024,512]{1,0:T(8,128)}, f32[1024,512]{1,0:T(8,128)}, /*index=5*/f32[512,1024]{1,0:T(8,128)}) custom-call(bf16[512,1024]{1,0:T(8,128)(2,1)} %get-tuple-element.15.mixed, bf16[512,1024]{1,0:T(8,128)(2,1)} %get-tuple-element.16.gin, ...), custom_call_target="tpu_custom_call" | custom-call | tf_op jit(solution)/shard_map/hand_over/pallas_call | solution.py:706

commit v7 on v6

--- a/solution.py
+++ b/solution.py
@@ -57,7 +57,8 @@
 
 
 def whole_kernel(
-    lens, tok_in, wk_in, wv_in, wq_in, cot_in, wo_in, mixed, gin, out,
+    lens, tok_in, wk_in, wv_in, wq_in, cot_in, wo_in, mixed_out, gin_out, total_out,
+    mixed, gin, out,
     tok, tokt, cot, wq, wk, wv, wo,
     kv, qg, summ, kvs, qgs, sums,
     kvt, gt, pair, pairt, sc, dsp, gkv, gsum, cg,
@@ -365,8 +366,16 @@
         rows = rows_of(i * 512, 512)
         return remote(qgs.at[i], rh.at[rows], s_bh.at[i], r_bh.at[i], behind)
 
-    def chunk(i, carry):
-        lax.fori_loop(i * (4 // UNROLL), (i + 1) * (4 // UNROLL), bar, 0)
+    def core_one(i):
+        @pl.when(c == 1)
+        def _():
+            rows = pl.ds(i * 512, 512)
+            qgs[i] = (gkv[rows, :] + rx[rows, :].astype(F32)).astype(BF)
+            halo_back(i).start()
+
+    def chunk(step, carry):
+        i = jnp.where(step == 1, 2, jnp.where(step == 2, 1, step))
+        lax.fori_loop(0, 4 // UNROLL, lambda u, kept: bar(i * (4 // UNROLL) + u, kept), 0)
 
         @pl.when(c == 0)
         def _():
@@ -374,15 +383,22 @@
             qgs[i] = gkv[rows, :].astype(BF)
             halo_back(i).start()
 
-        @pl.when(i >= 2)
-        def _():
-            cross(i - 2)
-            cross(i)
+        @pl.when(step == 1)
+        def _():
+            cross(0)
+
+        @pl.when(step == 2)
+        def _():
+            cross(2)
+            crossing(0).wait_recv()
+            core_one(0)
 
         give_back(cg, ret_cg, s_cg, r_cg, i)
         return carry
 
     lax.fori_loop(0, 4, chunk, 0)
+    cross(1)
+    cross(3)
     gss[...] = gsum[...].astype(BF).reshape(8, 16, 256)
     gsr[group] = gss[group]
     back_copies = []
@@ -395,14 +411,9 @@
         copy.start()
         back_copies.append(copy)
     turns = (0, 2, 1, 3)
-    for i in turns:
+    for i in turns[1:]:
         crossing(i).wait_recv()
-
-        @pl.when(c == 1)
-        def _():
-            rows = pl.ds(i * 512, 512)
-            qgs[i] = (gkv[rows, :] + rx[rows, :].astype(F32)).astype(BF)
-            halo_back(i).start()
+        core_one(i)
 
     def flatten(src, lane, n):
         for h in range(HEADS):
@@ -558,17 +569,20 @@
         return carry
 
     lax.fori_loop(0, 2, mix, 0)
-    advance(0, 0)
-    advance(3, 0)
+    mixed_written = pltpu.make_async_copy(mixed, mixed_out, s_in.at[0])
+    mixed_written.start()
+    for level in (0, 1):
+        advance(0, level)
+        advance(3, level)
     returned(qg, ret_kv, s_bkv, r_bkv)
     flatten(ret_kv, 0, 1)
     weight_grad(1, 1)
     flatten(ret_kv, TILE, 2)
     weight_grad(2, 2)
+    advance(0, 2)
+    advance(3, 2)
     begin(1)
     begin(2)
-    advance(0, 1)
-    advance(3, 1)
 
     def back(i, carry):
         rows = rows_of(i * 256, 256)
@@ -579,24 +593,32 @@
         return carry
 
     lax.fori_loop(0, 2, back, 0)
-    advance(0, 2)
-    advance(3, 2)
-    settled(0)
-    give(0, 0)
-    for level in (0, 1):
+    gin_written = pltpu.make_async_copy(gin, gin_out, s_in.at[1])
+    gin_written.start()
+    for m in (0, 3):
+        settled(m)
+        give(m, 0)
+    for level in range(3):
         advance(1, level)
         advance(2, level)
-    settled(3)
-    give(3, 0)
-    advance(1, 2)
-    advance(2, 2)
     finish(0)
+    finish(3)
     for m in (1, 2):
         settled(m)
         give(m, 0)
-    for m in (3, 1, 2):
-        finish(m)
-    for copy in last:
+    for n in range(2):
+        last[n].wait()
+    written = [pltpu.make_async_copy(out.at[m], total_out.at[m], s_in.at[2 + m]) for m in range(4)]
+    written[0].start()
+    written[3].start()
+    finish(1)
+    finish(2)
+    for n in (2, 3):
+        last[n].wait()
+        written[n - 1].start()
+    mixed_written.wait()
+    gin_written.wait()
+    for copy in written:
         copy.wait()
     for m in range(4):
         core_half(m).wait_send()
@@ -659,8 +681,9 @@
         whole_kernel,
         out_shape=(shape(512, 1024), shape(512, 1024), shape(4, 1024, 512)),
         in_specs=[SM] + [HB] * 6,
-        out_specs=(VM, VM, VM),
-        scratch_shapes=[vm((512, 1024), BF), vm((1024, 512), BF), vm((512, 1024), BF)]
+        out_specs=(HB, HB, HB),
+        scratch_shapes=[vm((512, 1024), BF), vm((512, 1024), BF), vm((4, 1024, 512), BF)]
+        + [vm((512, 1024), BF), vm((1024, 512), BF), vm((512, 1024), BF)]
         + [vm((1024, 512), BF)] * 3
         + [vm((512, 1024), BF), vm((6144, 256), BF)]
         + slabs(1)

time: 135 us -> 131 us (0.970)
  Pallas kernels: 135 us -> 130 us
    pallas_call x1, Pallas kernels: 129 us -> 124 us  [local(): pl.pallas_call(whole_kernel, out_shape=(shape(512, 1024), shape(512, 1024...]
where the time goes in v7:
time: 131 us; the launch traced here: 130 us
  Pallas kernels  130 us (99%)
    pallas_call x1, Pallas kernels, local(): pl.pallas_call(whole_kernel, out_shape=(shape(512, 1024), shape(512, 1024...  124 us
    pallas_call x1, Pallas kernels, local(): pl.pallas_call(hand_over, out_shape=(shape(512, 1024), shape(512, 1024))...  5.81 us

profile of v7, /device:TPU:1, one launch (start us, length us, event | category | flops | bytes accessed | tf_op | source)
XLA Modules:
  0.0 130.4 jit_solution(3656238653444663692)
XLA Ops:
  0.6 123.9 %whole.1 = (bf16[512,1024]{1,0:T(8,128)(2,1)}, bf16[512,1024]{1,0:T(8,128)(2,1)}, bf16[4,1024,512]{2,1,0:T(8,128)(2,1)}) custom-call(s32[1,128]{1,0:T(1,128)} %lens.1, bf16[512,1024]{1,0:T(8,128)(2,1)} %bitcast.4, bf16[1024,512]{1,0:T(8,128)(2,1)} %wk_in.1, bf16[1024,512]{1,0:T(8,128)(2,1)} %wv_in.1, bf16[1024,512]{1,0:T(8,128)(2,1)} %wq_in.1, ...), custom_call_target="tpu_custom_call" | custom-call | tf_op jit(solution)/shard_map/whole/pallas_call | solution.py:680
  124.6 5.8 %hand_over.1 = (bf16[512,1024]{1,0:T(8,128)(2,1)}, bf16[512,1024]{1,0:T(8,128)(2,1)}, f32[1024,512]{1,0:T(8,128)}, f32[1024,512]{1,0:T(8,128)}, f32[1024,512]{1,0:T(8,128)}, /*index=5*/f32[512,1024]{1,0:T(8,128)}) custom-call(bf16[512,1024]{1,0:T(8,128)(2,1)} %get-tuple-element.15.mixed, bf16[512,1024]{1,0:T(8,128)(2,1)} %get-tuple-element.16.gin, ...), custom_call_target="tpu_custom_call" | custom-call | tf_op jit(solution)/shard_map/hand_over/pallas_call | solution.py:729

commit v8 on v7

--- a/solution.py
+++ b/solution.py
@@ -542,7 +542,6 @@
     lax.fori_loop(0, 4, out_grad, 0)
     core_half(3).start()
     begin(0)
-    begin(3)
 
     for copy in back_copies:
         copy.wait()
@@ -563,6 +562,8 @@
             qg[rows, :] = ((total + jnp.where(live, share, 0.0)) * factor).astype(BF)
         give_back(qg, ret_kv, s_bkv, r_bkv, i)
 
+    begin(3)
+
     def mix(i, carry):
         rows = rows_of(i * 256, 256)
         mixed[rows, :] = jnp.dot(flat[3, rows, :], wo[...], preferred_element_type=F32).astype(BF)
@@ -571,16 +572,16 @@
     lax.fori_loop(0, 2, mix, 0)
     mixed_written = pltpu.make_async_copy(mixed, mixed_out, s_in.at[0])
     mixed_written.start()
-    for level in (0, 1):
-        advance(0, level)
-        advance(3, level)
+    advance(0, 0)
+    advance(0, 1)
+    advance(3, 0)
     returned(qg, ret_kv, s_bkv, r_bkv)
     flatten(ret_kv, 0, 1)
     weight_grad(1, 1)
     flatten(ret_kv, TILE, 2)
     weight_grad(2, 2)
     advance(0, 2)
-    advance(3, 2)
+    advance(3, 1)
     begin(1)
     begin(2)
 
@@ -595,6 +596,7 @@
     lax.fori_loop(0, 2, back, 0)
     gin_written = pltpu.make_async_copy(gin, gin_out, s_in.at[1])
     gin_written.start()
+    advance(3, 2)
     for m in (0, 3):
         settled(m)
         give(m, 0)
@@ -660,7 +662,7 @@
         copy.wait()
 
 
-ORDERS = ("yxz", "xzy", "zxy", "yzx")
+ORDERS = ("yxz", "zyx", "xzy", "xyz")
 UNROLL = 4
 
 HB = pl.BlockSpec(memory_space=pl.ANY)

time: 131 us -> 128 us (0.977)
  Pallas kernels: 130 us -> 127 us
    pallas_call x1, Pallas kernels: 124 us -> 121 us  [local(): pl.pallas_call(whole_kernel, out_shape=(shape(512, 1024), shape(512, 1024...]
where the time goes in v8:
time: 128 us; the launch traced here: 127 us
  Pallas kernels  127 us (99%)
    pallas_call x1, Pallas kernels, local(): pl.pallas_call(whole_kernel, out_shape=(shape(512, 1024), shape(512, 1024...  121 us
    pallas_call x1, Pallas kernels, local(): pl.pallas_call(hand_over, out_shape=(shape(512, 1024), shape(512, 1024))...  5.81 us

profile of v8, /device:TPU:1, one launch (start us, length us, event | category | flops | bytes accessed | tf_op | source)
XLA Modules:
  0.0 127.4 jit_solution(16060925665212538386)
XLA Ops:
  0.6 121.0 %whole.1 = (bf16[512,1024]{1,0:T(8,128)(2,1)}, bf16[512,1024]{1,0:T(8,128)(2,1)}, bf16[4,1024,512]{2,1,0:T(8,128)(2,1)}) custom-call(s32[1,128]{1,0:T(1,128)} %lens.1, bf16[512,1024]{1,0:T(8,128)(2,1)} %bitcast.4, bf16[1024,512]{1,0:T(8,128)(2,1)} %wk_in.1, bf16[1024,512]{1,0:T(8,128)(2,1)} %wv_in.1, bf16[1024,512]{1,0:T(8,128)(2,1)} %wq_in.1, ...), custom_call_target="tpu_custom_call" | custom-call | tf_op jit(solution)/shard_map/whole/pallas_call | solution.py:682
  121.6 5.8 %hand_over.1 = (bf16[512,1024]{1,0:T(8,128)(2,1)}, bf16[512,1024]{1,0:T(8,128)(2,1)}, f32[1024,512]{1,0:T(8,128)}, f32[1024,512]{1,0:T(8,128)}, f32[1024,512]{1,0:T(8,128)}, /*index=5*/f32[512,1024]{1,0:T(8,128)}) custom-call(bf16[512,1024]{1,0:T(8,128)(2,1)} %get-tuple-element.15.mixed, bf16[512,1024]{1,0:T(8,128)(2,1)} %get-tuple-element.16.gin, ...), custom_call_target="tpu_custom_call" | custom-call | tf_op jit(solution)/shard_map/hand_over/pallas_call | solution.py:731

commit v9 on v8

--- a/solution.py
+++ b/solution.py
@@ -235,12 +235,16 @@
         def _():
             across_copy(0, i).start()
 
-    lax.fori_loop(0, 16, prepare, 0)
+        lax.fori_loop(i * 4, i * 4 + 4, prepare, 0)
+
     for i in range(4):
-        across_copy(0, i).wait()
+        arrived(qgs, qg, 0, s_qg, r_qg, i)
+    for i in order:
+        across_copy(0, i).wait_recv()
+        lax.fori_loop(16 + i * 4, 20 + i * 4, prepare, 0)
+    for i in range(4):
+        across_copy(0, i).wait_send()
         halo_copy(i).wait_send()
-        arrived(qgs, qg, 0, s_qg, r_qg, i)
-    lax.fori_loop(16, 32, prepare, 0)
     for copy in sum_copies:
         copy.wait()
     kvt[:, 48 * TILE : 49 * TILE] = jnp.transpose(summ[...].reshape(TILE, 256))
@@ -294,17 +298,16 @@
             for j in range(count + 1):
                 here = slice(j * TILE, (j + 1) * TILE)
                 e = jnp.exp2(sc[u, here, :TILE] - tops[u])
-                sc[u, here, :TILE] = e
                 total = total + jnp.sum(e, axis=0, keepdims=True)
                 weighted = weighted + jnp.sum(e * sc[u, here, TILE:], axis=0, keepdims=True)
-            scales.append(1.0 / total)
-            deltas.append(weighted * scales[u])
+            scales.append(tops[u] + jnp.log(total) * LOG2E)
+            deltas.append(weighted / total)
         for u, qb in enumerate(ids):
             rows = rows_of(qb * TILE, TILE)
             both = pair[u]
             for j in range(count + 1):
                 here = slice(j * TILE, (j + 1) * TILE)
-                p = sc[u, here, :TILE] * scales[u]
+                p = jnp.exp2(sc[u, here, :TILE] - scales[u])
                 ds = (p * (sc[u, here, TILE:] - deltas[u])).astype(BF)
                 block = jnp.concatenate([ds, p.astype(BF)], axis=1)
                 dsp[u, here, :] = block
@@ -354,6 +357,44 @@
             def _():
                 remote(src.at[pl.ds(0, 512)], landing.at[h], send.at[0], recv.at[h], other).wait_recv()
 
+    def half_copy(i, h, to):
+        part = pl.ds(h * 256, 256)
+        return remote(
+            qg.at[pl.ds(i * 512 + h * 256, 256)], ret_kv.at[z, part], s_bkv.at[i, h], r_bkv.at[z, h], to
+        )
+
+    def give_half(i, h):
+        to, mine = owner(i)
+
+        @pl.when(mine)
+        def _():
+            ret_kv[z, h * 256 : h * 256 + 256] = qg[i * 512 + h * 256 : i * 512 + h * 256 + 256, :]
+
+        @pl.when(jnp.logical_not(mine))
+        def _():
+            half_copy(i, h, to).start()
+
+    def settle_halves():
+        for i in range(4):
+            to, mine = owner(i)
+
+            @pl.when(jnp.logical_not(mine))
+            def _():
+                for h in (0, 1):
+                    half_copy(i, h, to).wait_send()
+
+    def returned_halves():
+        part = [pl.ds(0, 256), pl.ds(256, 256)]
+        for n in range(HEADS):
+            mine = jnp.logical_and(z == n, at_home)
+
+            @pl.when(jnp.logical_not(mine))
+            def _():
+                for h in (0, 1):
+                    remote(
+                        qg.at[part[0]], ret_kv.at[n, part[h]], s_bkv.at[0, h], r_bkv.at[n, h], other
+                    ).wait_recv()
+
     def crossing(i):
         rows = rows_of(i * 512, 512)
         return remote(kvs.at[i], rx.at[rows], s_bx.at[i], r_bx.at[i], other)
@@ -362,16 +403,18 @@
         kvs[i] = gkv[rows_of(2048 + i * 512, 512), :].astype(BF)
         crossing(i).start()
 
-    def halo_back(i):
-        rows = rows_of(i * 512, 512)
-        return remote(qgs.at[i], rh.at[rows], s_bh.at[i], r_bh.at[i], behind)
+    def halo_back(i, h):
+        part = pl.ds(h * 256, 256)
+        rows = rows_of(i * 512 + h * 256, 256)
+        return remote(qgs.at[i, part], rh.at[rows], s_bh.at[i, h], r_bh.at[i, h], behind)
 
     def core_one(i):
         @pl.when(c == 1)
         def _():
             rows = pl.ds(i * 512, 512)
             qgs[i] = (gkv[rows, :] + rx[rows, :].astype(F32)).astype(BF)
-            halo_back(i).start()
+            for h in (0, 1):
+                halo_back(i, h).start()
 
     def chunk(step, carry):
         i = jnp.where(step == 1, 2, jnp.where(step == 2, 1, step))
@@ -381,7 +424,8 @@
         def _():
             rows = rows_of(i * 512, 512)
             qgs[i] = gkv[rows, :].astype(BF)
-            halo_back(i).start()
+            for h in (0, 1):
+                halo_back(i, h).start()
 
         @pl.when(step == 1)
         def _():
@@ -550,9 +594,9 @@
         coarse = coarse + gsr[n].astype(F32)
     lane = lax.broadcasted_iota(jnp.int32, (1, 256), 1)
     factor = jnp.where(lane < TILE, SCALE, 1.0)
-    for i in turns:
-        halo_back(i).wait_recv()
-        for b in range(4 * i, 4 * i + 4):
+    for i, h in [(i, h) for i in turns for h in (0, 1)]:
+        halo_back(i, h).wait_recv()
+        for b in (4 * i + 2 * h, 4 * i + 2 * h + 1):
             rows = pl.ds(b * TILE, TILE)
             length = lens[0, group * 16 + b]
             live = lax.broadcasted_iota(jnp.int32, (TILE, 256), 0) < length
@@ -560,7 +604,7 @@
             extra = jnp.where(c == 0, rx[rows, :].astype(F32), 0.0)
             total = gkv[pl.ds(OWN + b * TILE, TILE), :] + rh[rows, :].astype(F32) + extra
             qg[rows, :] = ((total + jnp.where(live, share, 0.0)) * factor).astype(BF)
-        give_back(qg, ret_kv, s_bkv, r_bkv, i)
+        give_half(i, h)
 
     begin(3)
 
@@ -575,7 +619,7 @@
     advance(0, 0)
     advance(0, 1)
     advance(3, 0)
-    returned(qg, ret_kv, s_bkv, r_bkv)
+    returned_halves()
     flatten(ret_kv, 0, 1)
     weight_grad(1, 1)
     flatten(ret_kv, TILE, 2)
@@ -625,11 +669,12 @@
     for m in range(4):
         core_half(m).wait_send()
         crossing(m).wait_send()
-        halo_back(m).wait_send()
+        for h in (0, 1):
+            halo_back(m, h).wait_send()
     for copy in started:
         copy.wait_send()
     settle(cg, ret_cg, s_cg, r_cg)
-    settle(qg, ret_kv, s_bkv, r_bkv)
+    settle_halves()
 
 
 def hand_over(mixed, gin, total, *refs):
@@ -718,7 +763,10 @@
         + [DMA((6,))]
         + [DMA((4,))] * 8
         + [DMA((8,))] * 2
-        + [DMA((4,))] * 8
+        + [DMA((4, 2))] * 2
+        + [DMA((4,))] * 2
+        + [DMA((4, 2))] * 2
+        + [DMA((4,))] * 2
         + [DMA((8,))] * 2
         + [DMA((2, 4))] * 2
         + [DMA((3, 4, 3))] * 2

time: 128 us -> 128 us (level)
  no operation moved by 1% of the time
where the time goes in v9:
time: 128 us; the launch traced here: 127 us
  Pallas kernels  127 us (99%)
    pallas_call x1, Pallas kernels, local(): pl.pallas_call(whole_kernel, out_shape=(shape(512, 1024), shape(512, 1024...  121 us
    pallas_call x1, Pallas kernels, local(): pl.pallas_call(hand_over, out_shape=(shape(512, 1024), shape(512, 1024))...  5.81 us

profile of v9, /device:TPU:1, one launch (start us, length us, event | category | flops | bytes accessed | tf_op | source)
XLA Modules:
  0.0 127.4 jit_solution(15101370386606147480)
XLA Ops:
  0.6 121.0 %whole.1 = (bf16[512,1024]{1,0:T(8,128)(2,1)}, bf16[512,1024]{1,0:T(8,128)(2,1)}, bf16[4,1024,512]{2,1,0:T(8,128)(2,1)}) custom-call(s32[1,128]{1,0:T(1,128)} %lens.1, bf16[512,1024]{1,0:T(8,128)(2,1)} %bitcast.4, bf16[1024,512]{1,0:T(8,128)(2,1)} %wk_in.1, bf16[1024,512]{1,0:T(8,128)(2,1)} %wv_in.1, bf16[1024,512]{1,0:T(8,128)(2,1)} %wq_in.1, ...), custom_call_target="tpu_custom_call" | custom-call | tf_op jit(solution)/shard_map/whole/pallas_call | solution.py:727
  121.6 5.8 %hand_over.1 = (bf16[512,1024]{1,0:T(8,128)(2,1)}, bf16[512,1024]{1,0:T(8,128)(2,1)}, f32[1024,512]{1,0:T(8,128)}, f32[1024,512]{1,0:T(8,128)}, f32[1024,512]{1,0:T(8,128)}, /*index=5*/f32[512,1024]{1,0:T(8,128)}) custom-call(bf16[512,1024]{1,0:T(8,128)(2,1)} %get-tuple-element.15.mixed, bf16[512,1024]{1,0:T(8,128)(2,1)} %get-tuple-element.16.gin, ...), custom_call_target="tpu_custom_call" | custom-call | tf_op jit(solution)/shard_map/hand_over/pallas_call | solution.py:779

commit v10 on v9

--- a/solution.py
+++ b/solution.py
@@ -66,7 +66,7 @@
     wg, got0, w0, got1, w1, got2, got3,
     s_in, s_kv, r_kv, s_qg, r_qg, s_h, r_h, s_x, r_x, s_s, r_s,
     s_bkv, r_bkv, s_cg, r_cg, s_bh, r_bh, s_bx, r_bx, s_gs, r_gs,
-    s0, r0, s1, r1, s2, r2,
+    s0, r0, s1, r1, s2, r2, s3, r3,
 ):
     y, x, z, c = place()
     loads = []
@@ -467,7 +467,7 @@
     levels = ((w0, got1, 256), (w1, got2, 64))
     pending = [None] * 4
     started = []
-    last = []
+    last = [[], [], [], []]
 
     def along(axis, d):
         at = dict(where)
@@ -508,6 +508,8 @@
             )
             copy.start()
             copies.append(copy)
+        if level == 0:
+            hand_on(m, 0)
         pending[m] = copies
         started.extend(copies)
 
@@ -555,11 +557,17 @@
             pending[m] = copies
             started.extend(copies)
 
+    def hand_on(m, d):
+        rows = pl.ds(pl.multiple_of(turn(where[ORDERS[m][0]], 4 - d) * 256, 16), 256)
+        block = out.at[m, rows, half]
+        copy = remote(block, block, s3.at[m, d], r3.at[m, d], other)
+        copy.start()
+        last[m].append(copy)
+
     def finish(m):
-        settled(m)
-        copy = remote(out.at[m, :, half], out.at[m, :, half], s0.at[1, m], r0.at[1, m], other)
-        copy.start()
-        last.append(copy)
+        for d in (1, 2, 3):
+            pending[m][d - 1].wait_recv()
+            hand_on(m, d)
 
     def weight_grad(n, m):
         def part(i, carry):
@@ -652,16 +660,17 @@
     for m in (1, 2):
         settled(m)
         give(m, 0)
-    for n in range(2):
-        last[n].wait()
+    for copy in last[0] + last[3]:
+        copy.wait()
     written = [pltpu.make_async_copy(out.at[m], total_out.at[m], s_in.at[2 + m]) for m in range(4)]
     written[0].start()
     written[3].start()
     finish(1)
     finish(2)
-    for n in (2, 3):
-        last[n].wait()
-        written[n - 1].start()
+    for m in (1, 2):
+        for copy in last[m]:
+            copy.wait()
+        written[m].start()
     mixed_written.wait()
     gin_written.wait()
     for copy in written:
@@ -770,7 +779,8 @@
         + [DMA((8,))] * 2
         + [DMA((2, 4))] * 2
         + [DMA((3, 4, 3))] * 2
-        + [DMA((2, 4, 3))] * 2,
+        + [DMA((2, 4, 3))] * 2
+        + [DMA((4, 4))] * 2,
         compiler_params=pltpu.CompilerParams(
             collective_id=0, has_side_effects=True, vmem_limit_bytes=62 * MIB
         ),

time: 128 us -> 127 us (level)
  no operation moved by 1% of the time
where the time goes in v10:
time: 127 us
  Pallas kernels  127 us (100%)
    pallas_call x1, Pallas kernels, local(): pl.pallas_call(whole_kernel, out_shape=(shape(512, 1024), shape(512, 1024...  121 us
    pallas_call x1, Pallas kernels, local(): pl.pallas_call(hand_over, out_shape=(shape(512, 1024), shape(512, 1024))...  5.81 us

profile of v10, /device:TPU:1, one launch (start us, length us, event | category | flops | bytes accessed | tf_op | source)
XLA Modules:
  0.0 127.3 jit_solution(14514449589892008937)
XLA Ops:
  0.6 120.9 %whole.1 = (bf16[512,1024]{1,0:T(8,128)(2,1)}, bf16[512,1024]{1,0:T(8,128)(2,1)}, bf16[4,1024,512]{2,1,0:T(8,128)(2,1)}) custom-call(s32[1,128]{1,0:T(1,128)} %lens.1, bf16[512,1024]{1,0:T(8,128)(2,1)} %bitcast.4, bf16[1024,512]{1,0:T(8,128)(2,1)} %wk_in.1, bf16[1024,512]{1,0:T(8,128)(2,1)} %wv_in.1, bf16[1024,512]{1,0:T(8,128)(2,1)} %wq_in.1, ...), custom_call_target="tpu_custom_call" | custom-call | tf_op jit(solution)/shard_map/whole/pallas_call | solution.py:736
  121.5 5.8 %hand_over.1 = (bf16[512,1024]{1,0:T(8,128)(2,1)}, bf16[512,1024]{1,0:T(8,128)(2,1)}, f32[1024,512]{1,0:T(8,128)}, f32[1024,512]{1,0:T(8,128)}, f32[1024,512]{1,0:T(8,128)}, /*index=5*/f32[512,1024]{1,0:T(8,128)}) custom-call(bf16[512,1024]{1,0:T(8,128)(2,1)} %get-tuple-element.15.mixed, bf16[512,1024]{1,0:T(8,128)(2,1)} %get-tuple-element.16.gin, ...), custom_call_target="tpu_custom_call" | custom-call | tf_op jit(solution)/shard_map/hand_over/pallas_call | solution.py:789
